TPU v7x, 512 devices: a whole 4x4x16 slice. The times are simulated.
512 devices in a mesh: pipe: 4 (over z_hi), dp: 8 (over y, core), tensor: 16 (over z_lo, x).
Axes of the slice: x: 4, y: 4, z: 16 (z_hi: 4, z_lo: 4; z = z_hi * 4 + z_lo), core: 2. Of those that a mesh axis runs over, the one named last changes fastest.
Arguments:
- x_prev: float32 [4, 2, 384, 6144], P('pipe', None, 'tensor', 'dp'), may hold values from -6 to 6
- hid_cot: bfloat16 [4, 2, 384, 24576], P('pipe', None, 'dp', 'tensor'), may hold values from -1.1953125 to 1.1953125
- w_up: bfloat16 [4, 6144, 24576], P('pipe', 'dp', 'tensor'), may hold values from -0.078125 to 0.078125
Outputs:
- upstream_grad: bfloat16 [4, 2, 384, 6144], P('pipe', None, 'tensor', 'dp')
- grad_up: bfloat16 [4, 6144, 24576], P('pipe', 'dp', 'tensor')
All inputs are finite; a program needn't handle non-finite values. Where the computation divides by a largest or mean magnitude, that divisor is 1e-20 or more.
Results may differ from a plain program's by a relative error of at most 0.03.
Values may be sent and summed in bfloat16 or wider, within the bound.
No kernel may reach another device: no remote copies, remote signals or barrier semaphores. Data moves between devices by JAX's collectives and lax.ppermute only.
A program may use at most 64 MiB of HBM per device.

v0:
```python
import jax
import jax.numpy as jnp
from jax import lax
from jax.sharding import PartitionSpec as P

BLOCK = 128


eps_scale = 1e-06
gelu_coef = 0.7978845608028654
cubic_coef = 0.044715


def from_behind(value, axis, steps):
    count = lax.axis_size(axis)
    pairs = [(source, (source + steps) % count) for source in range(count)]
    return lax.ppermute(value, axis, pairs)


def gelu_slope(preact):
    tanh_arg = gelu_coef * (preact + cubic_coef * preact * preact * preact)
    tangent = jnp.tanh(tanh_arg)
    return 0.5 * (1.0 + tangent) + 0.5 * preact * (1.0 - tangent * tangent) * gelu_coef * (
        1.0 + 3.0 * cubic_coef * preact * preact
    )


def local(x_prev, hid_cot, w_up):
    count_micro = x_prev.shape[1]
    own_rows = x_prev.shape[2]
    local_width = x_prev.shape[3]
    blocks = x_prev[0].reshape(count_micro, own_rows, local_width // BLOCK, BLOCK)
    block_scale = (jnp.max(jnp.abs(blocks), axis=-1) + eps_scale).astype(jnp.bfloat16)
    coded_vals = (
        (blocks / block_scale[..., None].astype(jnp.float32))
        .astype(jnp.bfloat16)
        .reshape(count_micro, own_rows, local_width)
    )
    coded_in, scale_in = from_behind((coded_vals, block_scale), "pipe", 1)
    restored = (
        (
            coded_in.reshape(count_micro, own_rows, local_width // BLOCK, BLOCK).astype(jnp.float32)
            * scale_in[..., None].astype(jnp.float32)
        )
        .astype(jnp.bfloat16)
        .reshape(count_micro, own_rows, local_width)
    )
    features = lax.all_gather(restored, "tensor", axis=1, tiled=True)
    up_matrix = w_up[0]
    partial_value = jnp.einsum(
        "mtd,df->mtf", features, up_matrix, preferred_element_type=jnp.float32
    )
    preact = lax.psum_scatter(
        partial_value.astype(jnp.bfloat16), "dp", scatter_dimension=1, tiled=True
    ).astype(jnp.float32)
    back_local = (hid_cot[0].astype(jnp.float32) * gelu_slope(preact)).astype(jnp.bfloat16)
    back_all = lax.all_gather(back_local, "dp", axis=1, tiled=True)
    grad_local = jnp.einsum("mtd,mtf->df", features, back_all, preferred_element_type=jnp.float32)
    term = jnp.einsum("mtf,df->tmd", back_all, up_matrix, preferred_element_type=jnp.float32)
    summed = lax.psum_scatter(
        term.reshape(own_rows * lax.axis_size("tensor"), count_micro * local_width).astype(
            jnp.bfloat16
        ),
        "tensor",
        scatter_dimension=0,
        tiled=True,
    ).astype(jnp.float32)
    back_input = jnp.transpose(summed.reshape(own_rows, count_micro, local_width), (1, 0, 2))
    upstream = from_behind(back_input.astype(jnp.bfloat16), "pipe", -1)
    return (upstream[None], grad_local.astype(jnp.bfloat16)[None])


def solution(mesh):
    return jax.shard_map(
        local,
        mesh=mesh,
        in_specs=(
            P("pipe", None, "tensor", "dp"),
            P("pipe", None, "dp", "tensor"),
            P("pipe", "dp", "tensor"),
        ),
        out_specs=(P("pipe", None, "tensor", "dp"), P("pipe", "dp", "tensor")),
        check_vma=False,
    )
```

profile of v0, /device:TPU:16, one launch (start us, length us, event | category | flops | bytes accessed | tf_op | source)
XLA Modules:
  0.0 315.8 jit_solution(4702447454744439992)
XLA Ops:
  7.2 1.1 abs.10
  8.3 0.1 reduce_max.9
  8.5 0.1 div.11
  8.6 0.9 fusion.19
  9.6 9.1 %collective-permute-start = (bf16[2,24,768]{2,1,0:T(8,128)(2,1)S(1)}, bf16[2,24,768]{2,1,0:T(8,128)(2,1)S(1)}, u32[]{:S(2)}, u32[]{:S(2)}) collective-permute-start(bf16[2,24,768]{2,1,0:T(8,128)(2,1)S(1)} %fusion.19), channel_id=1, source_target_pairs={{0,128},{128,256},{256,384},{384,0},{1,129},{129,257},{257,385},{3... | collective-permute-start | bytes 221192 | tf_op jit(solution)/shard_map/ppermute | solution.py:17
  18.7 9.1 %collective-permute-start.1 = (bf16[2,24,6]{2,1,0:T(8,128)(2,1)S(1)}, bf16[2,24,6]{2,1,0:T(8,128)(2,1)S(1)}, u32[]{:S(2)}, u32[]{:S(2)}) collective-permute-start(bf16[2,24,6]{2,1,0:T(8,128)(2,1)S(1)} %add_convert_fusion), channel_id=1, source_target_pairs={{0,128},{128,256},{256,384},{384,0},{1,129},{129,257},{257,385},{3... | collective-permute-start | bytes 1736 | tf_op jit(solution)/shard_map/ppermute | solution.py:17
  27.8 1.4 collective-permute-done.1
  29.2 0.1 mul.56
  29.3 0.7 multiply_convert_fusion
  30.1 86.3 %all-gather.3.cloned.1.call-done = bf16[2,384,768]{2,1,0:T(8,128)(2,1)} async-done(((bf16[2,24,768]{2,1,0:T(8,128)(2,1)}), bf16[2,384,768]{2,1,0:T(8,128)(2,1)}) %all-gather.3.cloned.1.call-update) | async-done | bytes 1179664 | tf_op jit(solution)/shard_map/all_gather | solution.py:48
  116.4 4.7 %convolution_convert_fusion = bf16[2,384,1536]{2,1,0:T(8,128)(2,1)} fusion(bf16[2,384,768]{2,1,0:T(8,128)(2,1)} %all-gather.3.cloned.1.call-done, bf16[1,768,1536]{2,1,0:T(8,128)(2,1)S(1)} %copy-done), kind=kOutput, calls=%fused_computation.1 | convolution fusion | flops 1813118976 | bytes 5898240 | tf_op jit(solution)/shard_map/mtd,df->mtf/dot_general | solution.py:50
  121.1 35.3 %reduce-scatter.5.cloned.1.call-done = bf16[2,48,1536]{2,1,0:T(8,128)(2,1)} async-done(((bf16[2,384,1536]{2,1,0:T(8,128)(2,1)}), bf16[2,48,1536]{2,1,0:T(8,128)(2,1)}) %reduce-scatter.5.cloned.1.call-update) | async-done | bytes 294928 | tf_op jit(solution)/shard_map/reduce_scatter | solution.py:53
  156.4 2.1 fusion.17
  158.5 0.0 reduce-scatter.7.cloned.1.call-start
  158.6 37.0 %all-gather.5.cloned.1.call-done = bf16[2,384,1536]{2,1,0:T(8,128)(2,1)} async-done(((bf16[2,48,1536]{2,1,0:T(8,128)(2,1)}), bf16[2,384,1536]{2,1,0:T(8,128)(2,1)}) %all-gather.5.cloned.1.call-update) | async-done | bytes 2359312 | tf_op jit(solution)/shard_map/all_gather | solution.py:57
  195.6 4.7 %fusion.7 = bf16[384,2,768]{2,0,1:T(8,128)(2,1)} fusion(bf16[2,384,1536]{2,1,0:T(8,128)(2,1)} %all-gather.5.cloned.1.call-done, bf16[1,768,1536]{2,1,0:T(8,128)(2,1)S(1)} %copy-done), kind=kOutput, calls=%fused_computation.14 | convolution fusion | flops 1812529152 | bytes 5898240 | tf_op jit(solution)/shard_map/mtf,df->tmd/dot_general | solution.py:59
  200.3 1.7 copy.8
  202.0 1.5 copy.12
  203.5 92.5 %reduce-scatter.7.cloned.1.call-done = bf16[24,1536]{1,0:T(8,128)(2,1)} async-done(((bf16[384,1536]{1,0:T(8,128)(2,1)}), bf16[24,1536]{1,0:T(8,128)(2,1)}) %reduce-scatter.7.cloned.1.call-update) | async-done | bytes 73744
  296.0 1.1 copy.13
  297.1 0.2 copy.11
  297.3 5.9 %collective-permute-start.2 = (bf16[2,24,768]{2,0,1:T(2,128)(2,1)S(1)}, bf16[2,24,768]{2,0,1:T(2,128)(2,1)S(1)}, u32[]{:S(2)}, u32[]{:S(2)}) collective-permute-start(bf16[2,24,768]{2,0,1:T(2,128)(2,1)S(1)} %bitcast.38), channel_id=1, source_target_pairs={{0,384},{128,0},{256,128},{384,256},{1,385},{129,1},{257,129},{385... | collective-permute-start | bytes 221192 | tf_op jit(solution)/shard_map/ppermute | solution.py:17
  303.1 5.5 %fusion = bf16[1,768,1536]{2,1,0:T(8,128)(2,1)} fusion(bf16[2,384,768]{2,1,0:T(8,128)(2,1)} %all-gather.3.cloned.1.call-done, bf16[2,384,1536]{2,1,0:T(8,128)(2,1)} %all-gather.5.cloned.1.call-done), kind=kOutput, calls=%fused_computation.2 | convolution fusion | flops 1813118976 | bytes 5898240 | tf_op jit(solution)/shard_map/mtd,mtf->df/dot_general | solution.py:58
  308.6 0.6 copy.10
  (17 shorter events, 0.3 us)
Async XLA Ops:
  7.2 109.2 %copy-start = (bf16[1,768,1536]{2,1,0:T(8,128)(2,1)S(1)}, bf16[1,768,1536]{2,1,0:T(8,128)(2,1)}, u32[]{:S(2)}) copy-start(bf16[1,768,1536]{2,1,0:T(8,128)(2,1)} %param.5) | copy-start | bytes 7077892
  7.2 109.2 %all-gather.3.cloned.1.call-start = ((), (), s32[]{:S(2)}) async-start(), calls=%async_computation.2 | async-start | bytes 1253376 | tf_op jit(solution)/shard_map/all_gather | solution.py:48
  9.6 19.8 %collective-permute-start = (bf16[2,24,768]{2,1,0:T(8,128)(2,1)S(1)}, bf16[2,24,768]{2,1,0:T(8,128)(2,1)S(1)}, u32[]{:S(2)}, u32[]{:S(2)}) collective-permute-start(bf16[2,24,768]{2,1,0:T(8,128)(2,1)S(1)} %fusion.19), channel_id=1, source_target_pairs={{0,128},{128,256},{256,384},{384,0},{1,129},{129,257},{257,385},{3... | collective-permute-start | bytes 221192 | tf_op jit(solution)/shard_map/ppermute | solution.py:17
  18.7 10.5 %collective-permute-start.1 = (bf16[2,24,6]{2,1,0:T(8,128)(2,1)S(1)}, bf16[2,24,6]{2,1,0:T(8,128)(2,1)S(1)}, u32[]{:S(2)}, u32[]{:S(2)}) collective-permute-start(bf16[2,24,6]{2,1,0:T(8,128)(2,1)S(1)} %add_convert_fusion), channel_id=1, source_target_pairs={{0,128},{128,256},{256,384},{384,0},{1,129},{129,257},{257,385},{3... | collective-permute-start | bytes 1736 | tf_op jit(solution)/shard_map/ppermute | solution.py:17
  30.0 126.4 %reduce-scatter.5.cloned.1.call-start = ((), (), s32[]{:S(2)}) async-start(), calls=%async_computation.3 | async-start | bytes 2654208 | tf_op jit(solution)/shard_map/reduce_scatter | solution.py:53
  121.1 35.4 %copy-start.1 = (bf16[1,2,48,1536]{3,2,1,0:T(8,128)(2,1)S(1)}, bf16[1,2,48,1536]{3,2,1,0:T(8,128)(2,1)}, u32[]{:S(2)}) copy-start(bf16[1,2,48,1536]{3,2,1,0:T(8,128)(2,1)} %param.4) | copy-start | bytes 884740
  121.1 74.5 %all-gather.5.cloned.1.call-start = ((), (), s32[]{:S(2)}) async-start(), calls=%async_computation.4 | async-start | bytes 2654208 | tf_op jit(solution)/shard_map/all_gather | solution.py:57
  158.5 137.4 %reduce-scatter.7.cloned.1.call-start = ((), (), s32[]{:S(2)}) async-start(), calls=%async_computation.5 | async-start | bytes 1253376
  297.3 11.3 %collective-permute-start.2 = (bf16[2,24,768]{2,0,1:T(2,128)(2,1)S(1)}, bf16[2,24,768]{2,0,1:T(2,128)(2,1)S(1)}, u32[]{:S(2)}, u32[]{:S(2)}) collective-permute-start(bf16[2,24,768]{2,0,1:T(2,128)(2,1)S(1)} %bitcast.38), channel_id=1, source_target_pairs={{0,384},{128,0},{256,128},{384,256},{1,385},{129,1},{257,129},{385... | collective-permute-start | bytes 221192 | tf_op jit(solution)/shard_map/ppermute | solution.py:17
Sparse Core Ops, SparseCore 0:
  30.1 86.2 all-gather.2
  121.2 35.1 reduce-scatter.4
  159.1 36.4 all-gather.4
  203.6 92.3 reduce-scatter.6
where the time goes:
time: 316 us
  waiting for transfers between devices  253 us (80%)
  starting transfers between devices  24.2 us (8%)
  matrix products  14.8 us (5%)
  between operations  13.9 us (4%)
  local copies, waits for them, and re-layouts  5.39 us (2%)
  other arithmetic  4.89 us (2%)
    unnamed x5, waiting for transfers between devices  92.6 us
    all_gather x1, waiting for transfers between devices, local(): features = lax.all_gather(restored, 'tensor', axis=1, tiled=True)  86.3 us
    all_gather x1, waiting for transfers between devices, local(): back_all = lax.all_gather(back_local, 'dp', axis=1, tiled=True)  37 us
    reduce_scatter x1, waiting for transfers between devices, local(): lax.psum_scatter(partial_value.astype(jnp.bfloat16), 'dp', scatter_dimens...  35.3 us
    ppermute x3, starting transfers between devices, from_behind(): return lax.ppermute(value, axis, pairs)  24 us
  transfers between devices with their start and end apart: 7, of which 5 were waited for; matrix products, arithmetic and copies ran while one was open for 2% of the time, Pallas kernels for 0%

commit v1 on v0

v1 whole, which is shorter than its diff:
```python
import jax
import jax.numpy as jnp
from jax import lax
from jax.sharding import PartitionSpec as P

BLOCK = 128
CORES = 2


eps_scale = 1e-06
gelu_coef = 0.7978845608028654
cubic_coef = 0.044715


def from_behind(value, axis, steps):
    count = lax.axis_size(axis)
    pairs = [(source, (source + steps) % count) for source in range(count)]
    return lax.ppermute(value, axis, pairs)


def from_sibling(value):
    return lax.ppermute(value, "dp", [(d, d ^ 1) for d in range(lax.axis_size("dp"))])


def gelu_slope(preact):
    tanh_arg = gelu_coef * (preact + cubic_coef * preact * preact * preact)
    tangent = jnp.tanh(tanh_arg)
    return 0.5 * (1.0 + tangent) + 0.5 * preact * (1.0 - tangent * tangent) * gelu_coef * (
        1.0 + 3.0 * cubic_coef * preact * preact
    )


def exchange(value, axis, groups):
    return lax.all_to_all(value, axis, 0, 0, axis_index_groups=groups, tiled=False)


def gathered(value, axis, groups):
    return exchange(jnp.broadcast_to(value[None], (len(groups[0]), *value.shape)), axis, groups)


def dot(a, b, contract):
    return lax.dot_general(a, b, (contract, ((), ())), preferred_element_type=jnp.float32)


def local(x_prev, hid_cot, w_up):
    f32, bf16 = jnp.float32, jnp.bfloat16
    micro, own_rows, width = x_prev.shape[1:]
    n_dp, n_tensor = lax.axis_size("dp"), lax.axis_size("tensor")
    n_y = n_dp // CORES
    n_z = n_y
    n_x = n_tensor // n_z
    rows = micro * own_rows
    hidden = w_up.shape[2]
    half = hidden // CORES
    y_groups = [[y * CORES + c for y in range(n_y)] for c in range(CORES)]
    x_groups = [[z * n_x + x for x in range(n_x)] for z in range(n_z)]
    z_groups = [[z * n_x + x for z in range(n_z)] for x in range(n_x)]
    core = lax.axis_index("dp") % CORES

    blocks = x_prev[0].reshape(micro, own_rows, width // BLOCK, BLOCK)
    block_scale = (jnp.max(jnp.abs(blocks), axis=-1, keepdims=True) + eps_scale).astype(bf16).astype(f32)
    coded = (blocks / block_scale).astype(bf16)
    restored = (coded.astype(f32) * block_scale).astype(bf16).reshape(rows, width)
    received = from_behind(restored, "pipe", 1)

    cot = hid_cot[0].reshape(micro, n_x // CORES, own_rows, hidden).transpose(1, 0, 2, 3)
    cot = cot.reshape(n_x // CORES * rows, hidden)
    cot_own = lax.dynamic_slice_in_dim(cot, core * half, half, 1)
    cot_in = from_sibling(lax.dynamic_slice_in_dim(cot, (1 - core) * half, half, 1))
    cot_all = jnp.where(core == 0, jnp.concatenate([cot_own, cot_in]), jnp.concatenate([cot_in, cot_own]))

    w_own = lax.dynamic_slice_in_dim(w_up[0], core * half, half, 1)
    w_other = lax.dynamic_slice_in_dim(w_up[0], (1 - core) * half, half, 1)

    by_z = gathered(received, "tensor", z_groups)
    by_xz = gathered(by_z, "tensor", x_groups)
    features = by_xz.transpose(1, 0, 2, 3).reshape(n_z * n_x * rows, width)

    part_other = dot(features, w_other, ((1,), (0,))).astype(bf16)
    part_in = from_sibling(part_other)
    part_own = dot(features, w_own, ((1,), (0,))).astype(bf16)
    part = (part_own.astype(f32) + part_in.astype(f32)).astype(bf16)
    parts = exchange(part.reshape(n_y, n_x * rows, half), "dp", y_groups)
    preact = jnp.sum(parts.astype(f32), axis=0)
    back = (cot_all.astype(f32) * gelu_slope(preact)).astype(bf16)
    back_own = gathered(back, "dp", y_groups).reshape(n_z * n_x * rows, half)
    back_other = from_sibling(back_own)

    term = dot(back_own, w_own, ((1,), (1,))) + dot(back_other, w_other, ((1,), (1,)))
    term = term.astype(bf16).reshape(n_z, n_x, rows, width).transpose(1, 0, 2, 3)
    by_x = exchange(term, "tensor", x_groups)
    sum_x = jnp.sum(by_x.astype(f32), axis=0).astype(bf16)
    by_z = exchange(sum_x, "tensor", z_groups)
    back_input = jnp.sum(by_z.astype(f32), axis=0).astype(bf16).reshape(micro, own_rows, width)
    upstream = from_behind(back_input, "pipe", -1)

    grad_own = dot(features, back_own, ((0,), (0,))).astype(bf16)
    grad_other = dot(features, back_other, ((0,), (0,))).astype(bf16)
    grad = jnp.where(
        core == 0,
        jnp.concatenate([grad_own, grad_other], 1),
        jnp.concatenate([grad_other, grad_own], 1),
    )
    return (upstream[None], grad[None])


def solution(mesh):
    return jax.shard_map(
        local,
        mesh=mesh,
        in_specs=(
            P("pipe", None, "tensor", "dp"),
            P("pipe", None, "dp", "tensor"),
            P("pipe", "dp", "tensor"),
        ),
        out_specs=(P("pipe", None, "tensor", "dp"), P("pipe", "dp", "tensor")),
        check_vma=False,
    )
```

time: 316 us -> 162 us (0.51)
  the two profiles are of different devices: /device:TPU:16 before, /device:TPU:1 now
where the time goes in v1:
time: 162 us; the launch traced here: 160 us
  blocking collectives  50.9 us (31%)
  starting transfers between devices  40.4 us (25%)
  waiting for transfers between devices  36.8 us (23%)
  matrix products  12.8 us (8%)
  local copies, waits for them, and re-layouts  9.77 us (6%)
  other arithmetic  8.55 us (5%)
    all_to_all x3, blocking collectives, exchange(): lax.all_to_all(value, axis, 0, 0, axis_index_groups=groups, tiled=False)  50.9 us
    all_to_all x3, waiting for transfers between devices, exchange(): lax.all_to_all(value, axis, 0, 0, axis_index_groups=groups, tiled=False)  27.2 us
    ppermute x2, starting transfers between devices, from_behind(): return lax.ppermute(value, axis, pairs)  14.1 us
    ppermute x3, starting transfers between devices, from_sibling(): lax.ppermute(value, 'dp', [(d, d ^ 1) for d in range(lax.axis_size('dp'))])  13.7 us
    dot_general x6, matrix products, dot(): lax.dot_general(a, b, (contract, ((), ())), preferred_element_type=jnp.fl...  12.8 us
    all_to_all x3, starting transfers between devices, exchange(): lax.all_to_all(value, axis, 0, 0, axis_index_groups=groups, tiled=False)  12.5 us
    unnamed x18, local copies, waits for them, and re-layouts  6.56 us
    ppermute x2, waiting for transfers between devices, from_behind(): return lax.ppermute(value, axis, pairs)  5.66 us
  transfers between devices with their start and end apart: 8, of which 6 were waited for; matrix products, arithmetic and copies ran while one was open for 10% of the time, Pallas kernels for 0%

profile of v1, /device:TPU:1, one launch (start us, length us, event | category | flops | bytes accessed | tf_op | source)
XLA Modules:
  0.0 160.1 jit_solution(14283988598039201459)
XLA Ops:
  2.1 9.6 %collective-permute-start.1 = (bf16[48,768]{1,0:T(8,128)(2,1)S(1)}, bf16[48,768]{1,0:T(8,128)(2,1)S(1)}, u32[]{:S(2)}, u32[]{:S(2)}) collective-permute-start(bf16[48,768]{1,0:T(8,128)(2,1)S(1)} %fusion.19), channel_id=1, source_target_pairs={{0,128},{128,256},{256,384},{384,0},{1,129},{129,257},{257,385},{3... | collective-permute-start | bytes 221192 | tf_op jit(solution)/shard_map/ppermute | solution.py:18
  11.8 5.7 %collective-permute-done.1 = bf16[48,768]{1,0:T(8,128)(2,1)S(1)} collective-permute-done((bf16[48,768]{1,0:T(8,128)(2,1)S(1)}, bf16[48,768]{1,0:T(8,128)(2,1)S(1)}, u32[]{:S(2)}, u32[]{:S(2)}) %collective-permute-start.1) | collective-permute-done | bytes 73760 | tf_op jit(solution)/shard_map/ppermute | solution.py:18
  17.4 14.9 %all_to_all.30 = bf16[4,48,768]{2,1,0:T(8,128)(2,1)S(1)} all-to-all(bf16[4,48,768]{2,1,0:T(8,128)(2,1)S(1)} %broadcast_in_dim.8), channel_id=1, replica_groups={{0,4,8,12},{1,5,9,13},{2,6,10,14},{3,7,11,15},{16,20,24,28},{17,21,25,2..., dimensions={0} | all-to-all | bytes 589824 | tf_op jit(solution)/shard_map/all_to_all | solution.py:34
  33.5 4.0 %all-to-all-start.1 = ((bf16[4,4,48,768]{3,2,1,0:T(8,128)(2,1)}), bf16[4,4,48,768]{3,2,1,0:T(8,128)(2,1)S(1)}, u32[]{:S(2)}, u32[]{:S(2)}) async-start(bf16[4,4,48,768]{3,2,1,0:T(8,128)(2,1)} %broadcast_in_dim.9), calls=%async_computation.1 | async-start | bytes 2359296 | tf_op jit(solution)/shard_map/all_to_all | solution.py:34
  37.5 12.6 %all-to-all-done.1 = bf16[4,4,48,768]{3,2,1,0:T(8,128)(2,1)S(1)} async-done(((bf16[4,4,48,768]{3,2,1,0:T(8,128)(2,1)}), bf16[4,4,48,768]{3,2,1,0:T(8,128)(2,1)S(1)}, u32[]{:S(2)}, u32[]{:S(2)}) %all-to-all-start.1) | async-done | bytes 1179680 | tf_op jit(solution)/shard_map/all_to_all | solution.py:34
  50.2 2.1 %convolution_convert_fusion.2 = bf16[768,768]{1,0:T(8,128)(2,1)} fusion(bf16[768,768]{1,0:T(8,128)(2,1)S(1)} %bitcast.55, bf16[1,768,1536]{2,1,0:T(8,128)(2,1)S(1)} %copy-done, s32[]{:T(128)S(6)} %select_n.45), kind=kOutput, calls=%fused_computation.6 | convolution fusion | flops 906559488 | bytes 3538948 | tf_op jit(solution)/shard_map/dot_general | solution.py:42
  52.3 6.7 %collective-permute-start.2 = (bf16[768,768]{1,0:T(8,128)(2,1)}, bf16[768,768]{1,0:T(8,128)(2,1)S(1)}, u32[]{:S(2)}, u32[]{:S(2)}) collective-permute-start(bf16[768,768]{1,0:T(8,128)(2,1)} %convolution_convert_fusion.2), channel_id=1, source_target_pairs={{0,16},{16,0},{32,48},{48,32},{64,80},{80,64},{96,112},{112,96},{1... | collective-permute-start | bytes 3538952 | tf_op jit(solution)/shard_map/ppermute | solution.py:22
  59.1 2.7 %collective-permute-done.2 = bf16[768,768]{1,0:T(8,128)(2,1)S(1)} collective-permute-done((bf16[768,768]{1,0:T(8,128)(2,1)}, bf16[768,768]{1,0:T(8,128)(2,1)S(1)}, u32[]{:S(2)}, u32[]{:S(2)}) %collective-permute-start.2) | collective-permute-done | bytes 1179680 | tf_op jit(solution)/shard_map/ppermute | solution.py:22
  61.7 3.4 %add_convert_fusion.1 = bf16[768,768]{1,0:T(8,128)(2,1)} fusion(bf16[768,768]{1,0:T(8,128)(2,1)S(1)} %collective-permute-done.2, bf16[768,768]{1,0:T(8,128)(2,1)} %bitcast.56, bf16[1,768,1536]{2,1,0:T(8,128)(2,1)S(1)} %copy-done, s32[]{:T(128)S(6)} %select_n.44), kind=kOutput, calls=%fused_computation.3 | convolution fusion | flops 908918784 | bytes 4718596 | tf_op jit(solution)/shard_map/dot_general | solution.py:42
  65.1 4.2 %all-to-all-start.2 = ((bf16[4,192,768]{2,1,0:T(8,128)(2,1)}), bf16[4,192,768]{2,1,0:T(8,128)(2,1)S(1)}, u32[]{:S(2)}, u32[]{:S(2)}) async-start(bf16[4,192,768]{2,1,0:T(8,128)(2,1)} %bitcast.62), calls=%async_computation.2 | async-start | bytes 2359296 | tf_op jit(solution)/shard_map/all_to_all | solution.py:34
  71.0 2.6 %collective-permute-start = (bf16[96,768]{1,0:T(8,128)(2,1)}, bf16[96,768]{1,0:T(8,128)(2,1)}, u32[]{:S(2)}, u32[]{:S(2)}) collective-permute-start(bf16[96,768]{1,0:T(8,128)(2,1)} %get-tuple-element.13), channel_id=1, source_target_pairs={{0,16},{16,0},{32,48},{48,32},{64,80},{80,64},{96,112},{112,96},{1... | collective-permute-start | bytes 442376 | tf_op jit(solution)/shard_map/ppermute | solution.py:22
  73.6 11.6 %all-to-all-done.2 = bf16[4,192,768]{2,1,0:T(8,128)(2,1)S(1)} async-done(((bf16[4,192,768]{2,1,0:T(8,128)(2,1)}), bf16[4,192,768]{2,1,0:T(8,128)(2,1)S(1)}, u32[]{:S(2)}, u32[]{:S(2)}) %all-to-all-start.2) | async-done | bytes 1179680 | tf_op jit(solution)/shard_map/all_to_all | solution.py:34
  87.6 17.3 %all_to_all.31 = bf16[4,192,768]{2,1,0:T(8,128)(2,1)S(1)} all-to-all(bf16[4,192,768]{2,1,0:T(8,128)(2,1)S(1)} %broadcast_in_dim.10), channel_id=1, replica_groups={{0,32,64,96},{16,48,80,112},{1,33,65,97},{17,49,81,113},{2,34,66,98},{1..., dimensions={0} | all-to-all | bytes 2359296 | tf_op jit(solution)/shard_map/all_to_all | solution.py:34
  104.9 4.5 %collective-permute-start.3 = (bf16[768,768]{1,0:T(8,128)(2,1)S(1)}, bf16[768,768]{1,0:T(8,128)(2,1)S(1)}, u32[]{:S(2)}, u32[]{:S(2)}) collective-permute-start(bf16[768,768]{1,0:T(8,128)(2,1)S(1)} %bitcast.59), channel_id=1, source_target_pairs={{0,16},{16,0},{32,48},{48,32},{64,80},{80,64},{96,112},{112,96},{1... | collective-permute-start | bytes 3538952 | tf_op jit(solution)/shard_map/ppermute | solution.py:22
  113.1 18.7 %all_to_all.32 = bf16[4,4,48,768]{3,2,1,0:T(8,128)(2,1)S(1)} all-to-all(bf16[4,4,48,768]{3,2,1,0:T(8,128)(2,1)S(1)} %bitcast.54), channel_id=1, replica_groups={{0,1,2,3},{4,5,6,7},{8,9,10,11},{12,13,14,15},{16,17,18,19},{20,21,22,2..., dimensions={0} | all-to-all | bytes 2359296 | tf_op jit(solution)/shard_map/all_to_all | solution.py:34
  132.7 4.3 %all-to-all-start.5 = ((bf16[4,48,768]{2,1,0:T(8,128)(2,1)}), bf16[4,48,768]{2,1,0:T(8,128)(2,1)}, u32[]{:S(2)}, u32[]{:S(2)}) async-start(bf16[4,48,768]{2,1,0:T(8,128)(2,1)} %reduce_sum.34), calls=%async_computation.5 | async-start | bytes 589824 | tf_op jit(solution)/shard_map/all_to_all | solution.py:34
  137.1 2.9 %fusion = bf16[1,768,768]{1,2,0:T(8,128)(2,1)S(1)} fusion(bf16[768,768]{1,0:T(8,128)(2,1)} %bitcast.57, bf16[768,768]{1,0:T(8,128)(2,1)} %bitcast.61), kind=kOutput, calls=%fused_computation.8 | convolution fusion | flops 906559488 | bytes 3538944 | tf_op jit(solution)/shard_map/dot_general | solution.py:42
  140.0 2.2 %fusion.1 = bf16[1,768,768]{1,2,0:T(8,128)(2,1)} fusion(bf16[768,768]{1,0:T(8,128)(2,1)S(1)} %bitcast.58, bf16[768,768]{1,0:T(8,128)(2,1)S(1)} %copy-done.7), kind=kOutput, calls=%fused_computation.9 | convolution fusion | flops 906559488 | bytes 3538944 | tf_op jit(solution)/shard_map/dot_general | solution.py:42
  142.2 2.9 %all-to-all-done.5 = bf16[4,48,768]{2,1,0:T(8,128)(2,1)} async-done(((bf16[4,48,768]{2,1,0:T(8,128)(2,1)}), bf16[4,48,768]{2,1,0:T(8,128)(2,1)}, u32[]{:S(2)}, u32[]{:S(2)}) %all-to-all-start.5) | async-done | bytes 294944 | tf_op jit(solution)/shard_map/all_to_all | solution.py:34
  145.1 1.7 %reduce_sum.35 = bf16[48,768]{1,0:T(8,128)(2,1)} reduce(bf16[4,48,768]{2,1,0:T(8,128)(2,1)} %all-to-all-done.5, bf16[]{:T(256)} %constant.45.clone.1), dimensions={0}, to_apply=%region_3.4 | reduce | flops 110592 | bytes 368642 | tf_op jit(solution)/shard_map/reduce_sum | solution.py:94
  146.7 4.5 %collective-permute-start.4 = (bf16[2,24,768]{2,1,0:T(8,128)(2,1)}, bf16[2,24,768]{2,1,0:T(8,128)(2,1)}, u32[]{:S(2)}, u32[]{:S(2)}) collective-permute-start(bf16[2,24,768]{2,1,0:T(8,128)(2,1)} %bitcast.67), channel_id=1, source_target_pairs={{0,384},{128,0},{256,128},{384,256},{1,385},{129,1},{257,129},{385... | collective-permute-start | bytes 221192 | tf_op jit(solution)/shard_map/ppermute | solution.py:18
  151.2 3.1 %maximum_select_fusion = bf16[1,768,1536]{1,2,0:T(8,128)(2,1)} fusion(bf16[1,768,768]{1,2,0:T(8,128)(2,1)} %fusion.1, bf16[1,768,768]{1,2,0:T(8,128)(2,1)S(1)} %fusion, pred[]{:T(512)S(6)} %eq.6), kind=kLoop, calls=%fused_computation | loop fusion | flops 10616832 | bytes 4718593 | tf_op jit(solution)/shard_map/jit(_where)/select_n | solution.py:99
  154.3 4.3 %copy.16 = bf16[1,768,1536]{2,1,0:T(8,128)(2,1)} copy(bf16[1,768,1536]{1,2,0:T(8,128)(2,1)} %maximum_select_fusion) | data formatting | bytes 4718592
  158.6 1.5 copy.25
  (37 shorter events, 11.3 us)
Async XLA Ops:
  0.6 49.6 %copy-start = (bf16[1,768,1536]{2,1,0:T(8,128)(2,1)S(1)}, bf16[1,768,1536]{2,1,0:T(8,128)(2,1)}, u32[]{:S(2)}) copy-start(bf16[1,768,1536]{2,1,0:T(8,128)(2,1)} %param.5) | copy-start | bytes 7077892
  0.6 1.4 copy-start.4
  2.1 15.3 %collective-permute-start.1 = (bf16[48,768]{1,0:T(8,128)(2,1)S(1)}, bf16[48,768]{1,0:T(8,128)(2,1)S(1)}, u32[]{:S(2)}, u32[]{:S(2)}) collective-permute-start(bf16[48,768]{1,0:T(8,128)(2,1)S(1)} %fusion.19), channel_id=1, source_target_pairs={{0,128},{128,256},{256,384},{384,0},{1,129},{129,257},{257,385},{3... | collective-permute-start | bytes 221192 | tf_op jit(solution)/shard_map/ppermute | solution.py:18
  33.5 16.6 %all-to-all-start.1 = ((bf16[4,4,48,768]{3,2,1,0:T(8,128)(2,1)}), bf16[4,4,48,768]{3,2,1,0:T(8,128)(2,1)S(1)}, u32[]{:S(2)}, u32[]{:S(2)}) async-start(bf16[4,4,48,768]{3,2,1,0:T(8,128)(2,1)} %broadcast_in_dim.9), calls=%async_computation.1 | async-start | bytes 2359296 | tf_op jit(solution)/shard_map/all_to_all | solution.py:34
  50.2 2.1 %copy-start.1 = (bf16[4,4,48,768]{3,2,0,1:T(8,128)(2,1)}, bf16[4,4,48,768]{3,2,0,1:T(8,128)(2,1)S(1)}, u32[]{:S(2)}) copy-start(bf16[4,4,48,768]{3,2,0,1:T(8,128)(2,1)S(1)} %copy.14) | copy-start | bytes 3538948
  52.3 9.4 %collective-permute-start.2 = (bf16[768,768]{1,0:T(8,128)(2,1)}, bf16[768,768]{1,0:T(8,128)(2,1)S(1)}, u32[]{:S(2)}, u32[]{:S(2)}) collective-permute-start(bf16[768,768]{1,0:T(8,128)(2,1)} %convolution_convert_fusion.2), channel_id=1, source_target_pairs={{0,16},{16,0},{32,48},{48,32},{64,80},{80,64},{96,112},{112,96},{1... | collective-permute-start | bytes 3538952 | tf_op jit(solution)/shard_map/ppermute | solution.py:22
  65.1 20.1 %all-to-all-start.2 = ((bf16[4,192,768]{2,1,0:T(8,128)(2,1)}), bf16[4,192,768]{2,1,0:T(8,128)(2,1)S(1)}, u32[]{:S(2)}, u32[]{:S(2)}) async-start(bf16[4,192,768]{2,1,0:T(8,128)(2,1)} %bitcast.62), calls=%async_computation.2 | async-start | bytes 2359296 | tf_op jit(solution)/shard_map/all_to_all | solution.py:34
  71.0 14.4 %collective-permute-start = (bf16[96,768]{1,0:T(8,128)(2,1)}, bf16[96,768]{1,0:T(8,128)(2,1)}, u32[]{:S(2)}, u32[]{:S(2)}) collective-permute-start(bf16[96,768]{1,0:T(8,128)(2,1)} %get-tuple-element.13), channel_id=1, source_target_pairs={{0,16},{16,0},{32,48},{48,32},{64,80},{80,64},{96,112},{112,96},{1... | collective-permute-start | bytes 442376 | tf_op jit(solution)/shard_map/ppermute | solution.py:22
  85.2 0.9 copy-start.5
  104.9 5.6 %copy-start.3 = (bf16[4,192,768]{2,1,0:T(8,128)(2,1)}, bf16[4,192,768]{2,1,0:T(8,128)(2,1)S(1)}, u32[]{:S(2)}) copy-start(bf16[4,192,768]{2,1,0:T(8,128)(2,1)S(1)} %all_to_all.31) | copy-start | bytes 3538948
  104.9 6.9 %collective-permute-start.3 = (bf16[768,768]{1,0:T(8,128)(2,1)S(1)}, bf16[768,768]{1,0:T(8,128)(2,1)S(1)}, u32[]{:S(2)}, u32[]{:S(2)}) collective-permute-start(bf16[768,768]{1,0:T(8,128)(2,1)S(1)} %bitcast.59), channel_id=1, source_target_pairs={{0,16},{16,0},{32,48},{48,32},{64,80},{80,64},{96,112},{112,96},{1... | collective-permute-start | bytes 3538952 | tf_op jit(solution)/shard_map/ppermute | solution.py:22
  111.9 1.1 copy-start.6
  132.7 12.4 %all-to-all-start.5 = ((bf16[4,48,768]{2,1,0:T(8,128)(2,1)}), bf16[4,48,768]{2,1,0:T(8,128)(2,1)}, u32[]{:S(2)}, u32[]{:S(2)}) async-start(bf16[4,48,768]{2,1,0:T(8,128)(2,1)} %reduce_sum.34), calls=%async_computation.5 | async-start | bytes 589824 | tf_op jit(solution)/shard_map/all_to_all | solution.py:34
  137.1 2.9 %copy-start.2 = (bf16[4,4,48,768]{3,2,0,1:T(8,128)(2,1)S(1)}, bf16[4,4,48,768]{3,2,0,1:T(8,128)(2,1)}, u32[]{:S(2)}) copy-start(bf16[4,4,48,768]{3,2,0,1:T(8,128)(2,1)} %copy-done.1) | copy-start | bytes 3538948
  137.1 2.9 %copy-start.7 = (bf16[768,768]{1,0:T(8,128)(2,1)S(1)}, bf16[768,768]{1,0:T(8,128)(2,1)}, u32[]{:S(2)}) copy-start(bf16[768,768]{1,0:T(8,128)(2,1)} %copy-done.6) | copy-start | bytes 3538948
  146.7 11.8 %collective-permute-start.4 = (bf16[2,24,768]{2,1,0:T(8,128)(2,1)}, bf16[2,24,768]{2,1,0:T(8,128)(2,1)}, u32[]{:S(2)}, u32[]{:S(2)}) collective-permute-start(bf16[2,24,768]{2,1,0:T(8,128)(2,1)} %bitcast.67), channel_id=1, source_target_pairs={{0,384},{128,0},{256,128},{384,256},{1,385},{129,1},{257,129},{385... | collective-permute-start | bytes 221192 | tf_op jit(solution)/shard_map/ppermute | solution.py:18

commit v2 on v1

v2 whole, which is shorter than its diff:
```python
import jax
import jax.numpy as jnp
from jax import lax
from jax.experimental import pallas as pl
from jax.experimental.pallas import tpu as pltpu
from jax.sharding import PartitionSpec as P

BLOCK = 128
CORES = 2
LAG = 18


eps_scale = 1e-06
gelu_coef = 0.7978845608028654
cubic_coef = 0.044715


def section_shift(value, steps):
    n_pipe = lax.axis_size("pipe")
    return lax.ppermute(value, "pipe", [(s, (s + steps) % n_pipe) for s in range(n_pipe)])


def from_sibling(value):
    return lax.ppermute(value, "dp", [(d, d ^ 1) for d in range(lax.axis_size("dp"))])


def gelu_slope(preact):
    tanh_arg = gelu_coef * (preact + cubic_coef * preact * preact * preact)
    tangent = jnp.tanh(tanh_arg)
    return 0.5 * (1.0 + tangent) + 0.5 * preact * (1.0 - tangent * tangent) * gelu_coef * (
        1.0 + 3.0 * cubic_coef * preact * preact
    )


def exchange(value, axis, groups):
    return lax.all_to_all(value, axis, 0, 0, axis_index_groups=groups, tiled=False)


def gathered(value, axis, groups):
    return exchange(jnp.broadcast_to(value[None], (len(groups[0]), *value.shape)), axis, groups)


def dot(a, b, contract):
    return lax.dot_general(a, b, (contract, ((), ())), preferred_element_type=jnp.float32)


def forward_kernel(core_ref, by_xz_ref, own_ref, other_ref, part_ref, feat_ref):
    f32, bf16 = jnp.float32, jnp.bfloat16
    n_x, n_zc, rows, _ = by_xz_ref.shape
    core = core_ref[0]

    @pl.when(pl.program_id(0) == 0)
    def _():
        for side in range(CORES):
            block = core if side == 0 else 1 - core
            for z in range(n_zc // CORES):
                piece = [by_xz_ref[x, z * CORES + block].astype(f32) for x in range(n_x)]
                feat_ref[side, pl.ds(z * n_x * rows, n_x * rows)] = jnp.concatenate(piece).astype(bf16)

    part = jnp.dot(feat_ref[0], own_ref[...], preferred_element_type=f32)
    part += jnp.dot(feat_ref[1], other_ref[...], preferred_element_type=f32)
    part_ref[...] = part.astype(bf16).reshape(part_ref.shape)


def forward(core, by_xz, w_own, w_other, tile):
    n_x, n_zc, rows, width = by_xz.shape
    hidden = w_own.shape[1]
    n_z = n_zc // CORES
    tokens = n_z * n_x * rows
    whole = lambda shape: pl.BlockSpec(shape, lambda j, _: (0,) * len(shape))
    weights = pl.BlockSpec((width, tile), lambda j, _: (0, j))
    return pl.pallas_call(
        forward_kernel,
        out_shape=(
            jax.ShapeDtypeStruct((n_z, n_x * rows, hidden), jnp.bfloat16),
            jax.ShapeDtypeStruct((CORES, tokens, width), jnp.bfloat16),
        ),
        grid_spec=pltpu.PrefetchScalarGridSpec(
            num_scalar_prefetch=1,
            grid=(hidden // tile,),
            in_specs=[whole(by_xz.shape), weights, weights],
            out_specs=(
                pl.BlockSpec((n_z, n_x * rows, tile), lambda j, _: (0, 0, j)),
                whole((CORES, tokens, width)),
            ),
        ),
        compiler_params=pltpu.CompilerParams(vmem_limit_bytes=40 * 2**20),
        cost_estimate=pl.CostEstimate(
            flops=2 * tokens * CORES * width * hidden, bytes_accessed=10 * 2**20, transcendentals=0
        ),
    )(core, by_xz, w_own, w_other)


def backward_kernel(core_ref, back_ref, own_ref, other_ref, term_ref):
    n_x, n_zc, rows, _ = term_ref.shape
    core = core_ref[0]
    for side, w_ref in enumerate((own_ref, other_ref)):
        block = core if side == 0 else 1 - core
        term = dot(back_ref[...], w_ref[...], ((1,), (1,)))
        for z in range(n_zc // CORES):
            for x in range(n_x):
                first = (z * n_x + x) * rows
                term_ref[x, z * CORES + block] = term[first : first + rows].astype(jnp.bfloat16)


def backward(core, back, w_own, w_other, n_z, n_x, tile):
    tokens, hidden = back.shape
    width = w_own.shape[0]
    rows = tokens // n_z // n_x
    weights = pl.BlockSpec((tile, hidden), lambda j, _: (j, 0))
    shape = (n_x, n_z * CORES, rows, width)
    return pl.pallas_call(
        backward_kernel,
        out_shape=jax.ShapeDtypeStruct(shape, jnp.bfloat16),
        grid_spec=pltpu.PrefetchScalarGridSpec(
            num_scalar_prefetch=1,
            grid=(width // tile,),
            in_specs=[pl.BlockSpec((tokens, hidden), lambda j, _: (0, 0)), weights, weights],
            out_specs=pl.BlockSpec((*shape[:3], tile), lambda j, _: (0, 0, 0, j)),
        ),
        compiler_params=pltpu.CompilerParams(vmem_limit_bytes=40 * 2**20),
        cost_estimate=pl.CostEstimate(
            flops=2 * tokens * CORES * width * hidden, bytes_accessed=8 * 2**20, transcendentals=0
        ),
    )(core, back, w_own, w_other)


def local(x_prev, hid_cot, w_up):
    f32, bf16 = jnp.float32, jnp.bfloat16
    micro, own_rows, width = x_prev.shape[1:]
    n_dp, n_tensor = lax.axis_size("dp"), lax.axis_size("tensor")
    n_y = n_dp // CORES
    n_z = n_y
    n_x = n_tensor // n_z
    tokens = n_tensor * own_rows
    hidden = w_up.shape[2]
    y_groups = [[y * CORES + c for y in range(n_y)] for c in range(CORES)]
    x_groups = [[z * n_x + x for x in range(n_x)] for z in range(n_z)]
    zc_groups = [
        [(y * CORES + c) * n_tensor + z * n_x + x for z in range(n_z) for c in range(CORES)]
        for y in range(n_y)
        for x in range(n_x)
    ]
    core = lax.axis_index("dp") % CORES
    core_list = core.reshape(1).astype(jnp.int32)
    mine = lambda value: lax.dynamic_index_in_dim(value, core, 0, False)
    siblings = lambda value: lax.dynamic_index_in_dim(value, 1 - core, 0, False)

    blocks = x_prev[0].reshape(micro, own_rows, width // BLOCK, BLOCK)
    block_scale = (jnp.max(jnp.abs(blocks), axis=-1, keepdims=True) + eps_scale).astype(bf16).astype(f32)
    coded = (blocks / block_scale).astype(bf16)
    restored = (coded.astype(f32) * block_scale).astype(bf16).reshape(micro, own_rows, width)
    received = section_shift(restored, 1)

    restored_c, cot = lax.optimization_barrier((restored, hid_cot[0]))
    cot_in = from_sibling(siblings(cot))
    cot_in, w_own = lax.optimization_barrier((cot_in, w_up[0]))
    w_other = from_sibling(w_own)
    cot_own = mine(cot)
    cot_all = jnp.where(core == 0, jnp.concatenate([cot_own, cot_in]), jnp.concatenate([cot_in, cot_own]))

    sent = jnp.broadcast_to(received[None], (n_z, micro, own_rows, width)).reshape(-1, own_rows, width)
    by_z = exchange(sent, ("dp", "tensor"), zc_groups)
    by_z = lax.fori_loop(0, (1 - core) * LAG, lambda i, v: jnp.maximum(v, -jnp.abs(v)), by_z)
    by_xz = gathered(by_z, "tensor", x_groups)
    part, features = forward(core_list, by_xz, w_own, w_other, 256)
    parts = exchange(part, "dp", y_groups)
    preact = jnp.sum(parts.astype(f32), axis=0)
    back = (cot_all.astype(f32) * gelu_slope(preact)).astype(bf16)
    back_all = gathered(back, "dp", y_groups).reshape(tokens, hidden)

    term = backward(core_list, back_all, w_own, w_other, n_z, n_x, 256)
    sum_x = jnp.sum(exchange(term, "tensor", x_groups).astype(f32), axis=0).astype(bf16)
    returned = exchange(sum_x, ("dp", "tensor"), zc_groups).reshape(n_z, micro, own_rows, width)
    back_input = jnp.sum(returned.astype(f32), axis=0).astype(bf16)
    upstream = section_shift(back_input, -1)

    back_late, _ = lax.optimization_barrier((back_all, term))
    grad_other = dot(features[1], back_late, ((0,), (0,))).astype(bf16)
    grad_other, _ = lax.optimization_barrier((grad_other, back_input))
    grad_in = from_sibling(grad_other)
    grad = (dot(features[0], back_late, ((0,), (0,))) + grad_in.astype(f32)).astype(bf16)
    upstream, grad = lax.optimization_barrier((upstream, grad))
    return (upstream[None], grad[None])


def solution(mesh):
    return jax.shard_map(
        local,
        mesh=mesh,
        in_specs=(
            P("pipe", None, "tensor", "dp"),
            P("pipe", None, "dp", "tensor"),
            P("pipe", "dp", "tensor"),
        ),
        out_specs=(P("pipe", None, "tensor", "dp"), P("pipe", "dp", "tensor")),
        check_vma=False,
    )
```

time: 162 us -> 147 us (0.907)
  starting transfers between devices: 40.4 us -> 50.7 us
  blocking collectives: 50.9 us -> 40.7 us
  Pallas kernels: 0 us -> 10 us
  matrix products: 12.8 us -> 5.67 us
  waiting for transfers between devices: 36.8 us -> 30.5 us
  other arithmetic: 8.55 us -> 2.71 us
  local copies, waits for them, and re-layouts: 9.77 us -> 4.9 us
    all_to_all x3, starting transfers between devices: 12.5 us -> 26.7 us  [exchange(): lax.all_to_all(value, axis, 0, 0, axis_index_groups=groups, tiled=False)]
    all_to_all x3, blocking collectives: 50.9 us -> 40.7 us  [exchange(): lax.all_to_all(value, axis, 0, 0, axis_index_groups=groups, tiled=False)]
    pallas_call x0 -> x2, Pallas kernels: none -> 10 us  [the longest x1 6.04 us: forward(): pl.pallas_call(forward_kernel, out_shape=(jax.ShapeDtypeStruct((n_z, n_x...]
    all_to_all x3, waiting for transfers between devices: 27.2 us -> 19.7 us  [exchange(): lax.all_to_all(value, axis, 0, 0, axis_index_groups=groups, tiled=False)]
    dot_general x6 -> x2, matrix products: 12.8 us -> 5.67 us  [dot(): lax.dot_general(a, b, (contract, ((), ())), preferred_element_type=jnp.fl...]
    ppermute x3, starting transfers between devices: 13.7 us -> 6.95 us  [from_sibling(): lax.ppermute(value, 'dp', [(d, d ^ 1) for d in range(lax.axis_size('dp'))])]
    ppermute x2, waiting for transfers between devices: 5.66 us -> 9.43 us  [section_shift(): lax.ppermute(value, 'pipe', [(s, (s + steps) % n_pipe) for s in range(n_p...]
    unnamed x18 -> x17, local copies, waits for them, and re-layouts: 6.56 us -> 3.15 us
  transfers between devices with their start and end apart: 8 -> 8, of which waited for: 6 -> 6; matrix products, arithmetic and copies ran while one was open for 10% -> 4% of each run, Pallas kernels for 0% -> 0%
where the time goes in v2:
time: 147 us; the launch traced here: 146 us
  starting transfers between devices  50.7 us (34%)
  blocking collectives  40.7 us (28%)
  waiting for transfers between devices  30.5 us (21%)
  Pallas kernels  10 us (7%)
  matrix products  5.67 us (4%)
  local copies, waits for them, and re-layouts  4.9 us (3%)
  other arithmetic  2.71 us (2%)
    all_to_all x3, blocking collectives, exchange(): lax.all_to_all(value, axis, 0, 0, axis_index_groups=groups, tiled=False)  40.7 us
    all_to_all x3, starting transfers between devices, exchange(): lax.all_to_all(value, axis, 0, 0, axis_index_groups=groups, tiled=False)  26.7 us
    all_to_all x3, waiting for transfers between devices, exchange(): lax.all_to_all(value, axis, 0, 0, axis_index_groups=groups, tiled=False)  19.7 us
    ppermute x2, starting transfers between devices, section_shift(): lax.ppermute(value, 'pipe', [(s, (s + steps) % n_pipe) for s in range(n_p...  17 us
    ppermute x2, waiting for transfers between devices, section_shift(): lax.ppermute(value, 'pipe', [(s, (s + steps) % n_pipe) for s in range(n_p...  9.43 us
    ppermute x3, starting transfers between devices, from_sibling(): lax.ppermute(value, 'dp', [(d, d ^ 1) for d in range(lax.axis_size('dp'))])  6.95 us
    pallas_call x1, Pallas kernels, forward(): pl.pallas_call(forward_kernel, out_shape=(jax.ShapeDtypeStruct((n_z, n_x...  6.04 us
    dot_general x2, matrix products, dot(): lax.dot_general(a, b, (contract, ((), ())), preferred_element_type=jnp.fl...  5.67 us
  transfers between devices with their start and end apart: 8, of which 6 were waited for; matrix products, arithmetic and copies ran while one was open for 4% of the time, Pallas kernels for 0%

profile of v2, /device:TPU:1, one launch (start us, length us, event | category | flops | bytes accessed | tf_op | source)
XLA Modules:
  0.0 146.0 jit_solution(4128811352693480051)
XLA Ops:
  0.6 1.0 abs.13
  2.0 9.8 %collective-permute-start.1 = (bf16[2,24,768]{2,1,0:T(8,128)(2,1)S(1)}, bf16[2,24,768]{2,1,0:T(8,128)(2,1)S(1)}, u32[]{:S(2)}, u32[]{:S(2)}) collective-permute-start(bf16[2,24,768]{2,1,0:T(8,128)(2,1)S(1)} %multiply_convert_fusion), channel_id=1, source_target_pairs={{0,128},{128,256},{256,384},{384,0},{1,129},{129,257},{257,385},{3... | collective-permute-start | bytes 221192 | tf_op jit(solution)/shard_map/ppermute | solution.py:20
  11.8 5.7 %collective-permute-done.1 = bf16[2,24,768]{2,1,0:T(8,128)(2,1)S(1)} collective-permute-done((bf16[2,24,768]{2,1,0:T(8,128)(2,1)S(1)}, bf16[2,24,768]{2,1,0:T(8,128)(2,1)S(1)}, u32[]{:S(2)}, u32[]{:S(2)}) %collective-permute-start.1) | collective-permute-done | bytes 73760 | tf_op jit(solution)/shard_map/ppermute | solution.py:20
  18.2 9.1 %all-to-all-start = ((bf16[8,24,768]{2,1,0:T(8,128)(2,1)}), bf16[8,24,768]{2,1,0:T(8,128)(2,1)S(1)}, u32[]{:S(2)}, u32[]{:S(2)}) async-start(bf16[8,24,768]{2,1,0:T(8,128)(2,1)} %bitcast.6), calls=%async_computation | async-start | bytes 589824 | tf_op jit(solution)/shard_map/all_to_all | solution.py:36
  28.0 1.9 %collective-permute-start = (bf16[48,1536]{1,0:T(8,128)(2,1)S(1)}, bf16[48,1536]{1,0:T(8,128)(2,1)S(1)}, u32[]{:S(2)}, u32[]{:S(2)}) collective-permute-start(bf16[48,1536]{1,0:T(8,128)(2,1)S(1)} %get-tuple-element.46), channel_id=1, source_target_pairs={{0,16},{16,0},{32,48},{48,32},{64,80},{80,64},{96,112},{112,96},{1... | collective-permute-start | bytes 442376 | tf_op jit(solution)/shard_map/ppermute | solution.py:24
  29.9 1.3 collective-permute-done
  31.9 2.0 %collective-permute-start.2 = (bf16[768,1536]{1,0:T(8,128)(2,1)S(1)}, bf16[768,1536]{1,0:T(8,128)(2,1)}, u32[]{:S(2)}, u32[]{:S(2)}) collective-permute-start(bf16[768,1536]{1,0:T(8,128)(2,1)S(1)} %bitcast.31), channel_id=1, source_target_pairs={{0,16},{16,0},{32,48},{48,32},{64,80},{80,64},{96,112},{112,96},{1... | collective-permute-start | bytes 7077896 | tf_op jit(solution)/shard_map/ppermute | solution.py:24
  34.0 2.7 %all-to-all-done = bf16[8,24,768]{2,1,0:T(8,128)(2,1)S(1)} async-done(((bf16[8,24,768]{2,1,0:T(8,128)(2,1)}), bf16[8,24,768]{2,1,0:T(8,128)(2,1)S(1)}, u32[]{:S(2)}, u32[]{:S(2)}) %all-to-all-start) | async-done | bytes 294944 | tf_op jit(solution)/shard_map/all_to_all | solution.py:36
  36.8 14.9 %all_to_all.30.by_xz_ref = bf16[4,8,24,768]{3,2,1,0:T(8,128)(2,1)S(1)} all-to-all(bf16[4,8,24,768]{3,2,1,0:T(8,128)(2,1)S(1)} %broadcast_in_dim.11), channel_id=1, replica_groups={{0,1,2,3},{4,5,6,7},{8,9,10,11},{12,13,14,15},{16,17,18,19},{20,21,22,2..., dimensions={0} | all-to-all | bytes 2359296 | tf_op jit(solution)/shard_map/all_to_all | solution.py:36
  51.7 6.0 %shard_map.50 = (bf16[4,96,1536]{2,1,0:T(8,128)(2,1)}, bf16[2,384,768]{2,1,0:T(8,128)(2,1)S(1)}) custom-call(s32[1]{0:T(128)} %bitcast.core_ref, bf16[4,8,24,768]{3,2,1,0:T(8,128)(2,1)S(1)} %all_to_all.30.by_xz_ref, bf16[768,1536]{1,0:T(8,128)(2,1)S(1)} %bitcast.32, bf16[768,1536]{1,0:T(8,128)(2,1)} %collective-permute-done.2.other_ref), custom_call_target="tpu_custom_call" | custom-call | flops 1811939328 | bytes 10485760 | tf_op jit(solution)/shard_map/pallas_call | solution.py:72
  57.7 1.0 copy-done.1
  58.8 4.2 %all-to-all-start.2 = ((bf16[4,96,1536]{2,1,0:T(8,128)(2,1)}), bf16[4,96,1536]{2,1,0:T(8,128)(2,1)S(1)}, u32[]{:S(2)}, u32[]{:S(2)}) async-start(bf16[4,96,1536]{2,1,0:T(8,128)(2,1)} %get-tuple-element.33), calls=%async_computation.2 | async-start | bytes 2359296 | tf_op jit(solution)/shard_map/all_to_all | solution.py:36
  63.0 10.4 %all-to-all-done.2 = bf16[4,96,1536]{2,1,0:T(8,128)(2,1)S(1)} async-done(((bf16[4,96,1536]{2,1,0:T(8,128)(2,1)}), bf16[4,96,1536]{2,1,0:T(8,128)(2,1)S(1)}, u32[]{:S(2)}, u32[]{:S(2)}) %all-to-all-start.2) | async-done | bytes 1179680 | tf_op jit(solution)/shard_map/all_to_all | solution.py:36
  74.9 12.9 %all_to_all.31 = bf16[4,96,1536]{2,1,0:T(8,128)(2,1)S(1)} all-to-all(bf16[4,96,1536]{2,1,0:T(8,128)(2,1)S(1)} %broadcast_in_dim.12), channel_id=1, replica_groups={{0,32,64,96},{16,48,80,112},{1,33,65,97},{17,49,81,113},{2,34,66,98},{1..., dimensions={0} | all-to-all | bytes 2359296 | tf_op jit(solution)/shard_map/all_to_all | solution.py:36
  87.8 4.0 %shard_map.51 = bf16[4,8,24,768]{3,2,1,0:T(8,128)(2,1)S(1)} custom-call(s32[1]{0:T(128)} %bitcast.core_ref, bf16[384,1536]{1,0:T(8,128)(2,1)S(1)} %bitcast.28, bf16[768,1536]{1,0:T(8,128)(2,1)S(1)} %bitcast.33, bf16[768,1536]{1,0:T(8,128)(2,1)} %collective-permute-done.2.other_ref), custom_call_target="tpu_custom_call" | custom-call | flops 1811939328 | bytes 8388608 | tf_op jit(solution)/shard_map/pallas_call | solution.py:112
  91.8 12.9 %all_to_all.32 = bf16[4,8,24,768]{3,2,1,0:T(8,128)(2,1)S(1)} all-to-all(bf16[4,8,24,768]{3,2,1,0:T(8,128)(2,1)S(1)} %shard_map.51), channel_id=1, replica_groups={{0,1,2,3},{4,5,6,7},{8,9,10,11},{12,13,14,15},{16,17,18,19},{20,21,22,2..., dimensions={0} | all-to-all | bytes 2359296 | tf_op jit(solution)/shard_map/all_to_all | solution.py:36
  104.6 0.9 reduce_sum.34
  105.6 13.4 %all-to-all-start.5 = ((bf16[8,24,768]{2,1,0:T(8,128)(2,1)}), bf16[8,24,768]{2,1,0:T(8,128)(2,1)S(1)}, u32[]{:S(2)}, u32[]{:S(2)}) async-start(bf16[8,24,768]{2,1,0:T(8,128)(2,1)} %reduce_sum.34), calls=%async_computation.5 | async-start | bytes 589824 | tf_op jit(solution)/shard_map/all_to_all | solution.py:36
  119.0 2.8 %convolution_convert_fusion = bf16[768,1536]{1,0:T(8,128)(2,1)} fusion(bf16[384,1536]{1,0:T(8,128)(2,1)S(1)} %bitcast.29, bf16[2,384,768]{2,1,0:T(8,128)(2,1)S(1)} %copy-done.2), kind=kOutput, calls=%fused_computation.2 | convolution fusion | flops 907149312 | bytes 4128768 | tf_op jit(solution)/shard_map/dot_general | solution.py:44
  121.8 6.6 %all-to-all-done.5 = bf16[8,24,768]{2,1,0:T(8,128)(2,1)S(1)} async-done(((bf16[8,24,768]{2,1,0:T(8,128)(2,1)}), bf16[8,24,768]{2,1,0:T(8,128)(2,1)S(1)}, u32[]{:S(2)}, u32[]{:S(2)}) %all-to-all-start.5) | async-done | bytes 294944 | tf_op jit(solution)/shard_map/all_to_all | solution.py:36
  128.4 3.0 %collective-permute-start.4 = (bf16[768,1536]{1,0:T(8,128)(2,1)}, bf16[768,1536]{1,0:T(8,128)(2,1)S(1)}, u32[]{:S(2)}, u32[]{:S(2)}) collective-permute-start(bf16[768,1536]{1,0:T(8,128)(2,1)} %convolution_convert_fusion), channel_id=1, source_target_pairs={{0,16},{16,0},{32,48},{48,32},{64,80},{80,64},{96,112},{112,96},{1... | collective-permute-start | bytes 7077896 | tf_op jit(solution)/shard_map/ppermute | solution.py:24
  131.4 7.3 %collective-permute-start.3 = (bf16[2,24,768]{2,1,0:T(8,128)(2,1)S(1)}, bf16[2,24,768]{2,1,0:T(8,128)(2,1)S(1)}, u32[]{:S(2)}, u32[]{:S(2)}) collective-permute-start(bf16[2,24,768]{2,1,0:T(8,128)(2,1)S(1)} %reduce_sum.35), channel_id=1, source_target_pairs={{0,384},{128,0},{256,128},{384,256},{1,385},{129,1},{257,129},{385... | collective-permute-start | bytes 221192 | tf_op jit(solution)/shard_map/ppermute | solution.py:20
  138.7 2.8 %add_convert_fusion = bf16[768,1536]{1,0:T(8,128)(2,1)} fusion(bf16[768,1536]{1,0:T(8,128)(2,1)S(1)} %collective-permute-done.4, bf16[384,1536]{1,0:T(8,128)(2,1)S(1)} %bitcast.30, bf16[2,384,768]{2,1,0:T(8,128)(2,1)S(1)} %copy-done.2), kind=kOutput, calls=%fused_computation.1 | convolution fusion | flops 909508608 | bytes 6488064 | tf_op jit(solution)/shard_map/dot_general | solution.py:44
  141.6 3.8 %collective-permute-done.3 = bf16[2,24,768]{2,1,0:T(8,128)(2,1)S(1)} collective-permute-done((bf16[2,24,768]{2,1,0:T(8,128)(2,1)S(1)}, bf16[2,24,768]{2,1,0:T(8,128)(2,1)S(1)}, u32[]{:S(2)}, u32[]{:S(2)}) %collective-permute-start.3) | collective-permute-done | bytes 73760 | tf_op jit(solution)/shard_map/ppermute | solution.py:20
  (32 shorter events, 4.7 us)
Async XLA Ops:
  0.6 1.4 copy-start.3
  1.7 25.7 %copy-start.5 = (bf16[1,2,48,1536]{3,2,1,0:T(8,128)(2,1)S(1)}, bf16[1,2,48,1536]{3,2,1,0:T(8,128)(2,1)}, u32[]{:S(2)}) copy-start(bf16[1,2,48,1536]{3,2,1,0:T(8,128)(2,1)} %param.6) | copy-start | bytes 884740
  1.8 30.1 %copy-start = (bf16[1,768,1536]{2,1,0:T(8,128)(2,1)S(1)}, bf16[1,768,1536]{2,1,0:T(8,128)(2,1)}, u32[]{:S(2)}) copy-start(bf16[1,768,1536]{2,1,0:T(8,128)(2,1)} %param.7) | copy-start | bytes 7077892
  2.0 15.4 %collective-permute-start.1 = (bf16[2,24,768]{2,1,0:T(8,128)(2,1)S(1)}, bf16[2,24,768]{2,1,0:T(8,128)(2,1)S(1)}, u32[]{:S(2)}, u32[]{:S(2)}) collective-permute-start(bf16[2,24,768]{2,1,0:T(8,128)(2,1)S(1)} %multiply_convert_fusion), channel_id=1, source_target_pairs={{0,128},{128,256},{256,384},{384,0},{1,129},{129,257},{257,385},{3... | collective-permute-start | bytes 221192 | tf_op jit(solution)/shard_map/ppermute | solution.py:20
  18.2 18.5 %all-to-all-start = ((bf16[8,24,768]{2,1,0:T(8,128)(2,1)}), bf16[8,24,768]{2,1,0:T(8,128)(2,1)S(1)}, u32[]{:S(2)}, u32[]{:S(2)}) async-start(bf16[8,24,768]{2,1,0:T(8,128)(2,1)} %bitcast.6), calls=%async_computation | async-start | bytes 589824 | tf_op jit(solution)/shard_map/all_to_all | solution.py:36
  28.0 3.3 %collective-permute-start = (bf16[48,1536]{1,0:T(8,128)(2,1)S(1)}, bf16[48,1536]{1,0:T(8,128)(2,1)S(1)}, u32[]{:S(2)}, u32[]{:S(2)}) collective-permute-start(bf16[48,1536]{1,0:T(8,128)(2,1)S(1)} %get-tuple-element.46), channel_id=1, source_target_pairs={{0,16},{16,0},{32,48},{48,32},{64,80},{80,64},{96,112},{112,96},{1... | collective-permute-start | bytes 442376 | tf_op jit(solution)/shard_map/ppermute | solution.py:24
  31.3 0.7 copy-start.6
  31.9 19.8 %collective-permute-start.2 = (bf16[768,1536]{1,0:T(8,128)(2,1)S(1)}, bf16[768,1536]{1,0:T(8,128)(2,1)}, u32[]{:S(2)}, u32[]{:S(2)}) collective-permute-start(bf16[768,1536]{1,0:T(8,128)(2,1)S(1)} %bitcast.31), channel_id=1, source_target_pairs={{0,16},{16,0},{32,48},{48,32},{64,80},{80,64},{96,112},{112,96},{1... | collective-permute-start | bytes 7077896 | tf_op jit(solution)/shard_map/ppermute | solution.py:24
  57.7 1.0 copy-start.1
  58.8 14.6 %all-to-all-start.2 = ((bf16[4,96,1536]{2,1,0:T(8,128)(2,1)}), bf16[4,96,1536]{2,1,0:T(8,128)(2,1)S(1)}, u32[]{:S(2)}, u32[]{:S(2)}) async-start(bf16[4,96,1536]{2,1,0:T(8,128)(2,1)} %get-tuple-element.33), calls=%async_computation.2 | async-start | bytes 2359296 | tf_op jit(solution)/shard_map/all_to_all | solution.py:36
  73.4 0.9 copy-start.4
  73.4 1.0 copy-start.7
  104.6 14.4 %copy-start.2 = (bf16[2,384,768]{2,1,0:T(8,128)(2,1)S(1)}, bf16[2,384,768]{2,1,0:T(8,128)(2,1)}, u32[]{:S(2)}) copy-start(bf16[2,384,768]{2,1,0:T(8,128)(2,1)} %copy-done.1) | copy-start | bytes 3538948
  105.6 22.8 %all-to-all-start.5 = ((bf16[8,24,768]{2,1,0:T(8,128)(2,1)}), bf16[8,24,768]{2,1,0:T(8,128)(2,1)S(1)}, u32[]{:S(2)}, u32[]{:S(2)}) async-start(bf16[8,24,768]{2,1,0:T(8,128)(2,1)} %reduce_sum.34), calls=%async_computation.5 | async-start | bytes 589824 | tf_op jit(solution)/shard_map/all_to_all | solution.py:36
  128.4 10.3 %collective-permute-start.4 = (bf16[768,1536]{1,0:T(8,128)(2,1)}, bf16[768,1536]{1,0:T(8,128)(2,1)S(1)}, u32[]{:S(2)}, u32[]{:S(2)}) collective-permute-start(bf16[768,1536]{1,0:T(8,128)(2,1)} %convolution_convert_fusion), channel_id=1, source_target_pairs={{0,16},{16,0},{32,48},{48,32},{64,80},{80,64},{96,112},{112,96},{1... | collective-permute-start | bytes 7077896 | tf_op jit(solution)/shard_map/ppermute | solution.py:24
  131.4 13.9 %collective-permute-start.3 = (bf16[2,24,768]{2,1,0:T(8,128)(2,1)S(1)}, bf16[2,24,768]{2,1,0:T(8,128)(2,1)S(1)}, u32[]{:S(2)}, u32[]{:S(2)}) collective-permute-start(bf16[2,24,768]{2,1,0:T(8,128)(2,1)S(1)} %reduce_sum.35), channel_id=1, source_target_pairs={{0,384},{128,0},{256,128},{384,256},{1,385},{129,1},{257,129},{385... | collective-permute-start | bytes 221192 | tf_op jit(solution)/shard_map/ppermute | solution.py:20

commit v3 on v2

--- a/solution.py
+++ b/solution.py
@@ -84,7 +84,7 @@
                 whole((CORES, tokens, width)),
             ),
         ),
-        compiler_params=pltpu.CompilerParams(vmem_limit_bytes=40 * 2**20),
+        compiler_params=pltpu.CompilerParams(vmem_limit_bytes=16 * 2**20),
         cost_estimate=pl.CostEstimate(
             flops=2 * tokens * CORES * width * hidden, bytes_accessed=10 * 2**20, transcendentals=0
         ),
@@ -118,7 +118,7 @@
             in_specs=[pl.BlockSpec((tokens, hidden), lambda j, _: (0, 0)), weights, weights],
             out_specs=pl.BlockSpec((*shape[:3], tile), lambda j, _: (0, 0, 0, j)),
         ),
-        compiler_params=pltpu.CompilerParams(vmem_limit_bytes=40 * 2**20),
+        compiler_params=pltpu.CompilerParams(vmem_limit_bytes=16 * 2**20),
         cost_estimate=pl.CostEstimate(
             flops=2 * tokens * CORES * width * hidden, bytes_accessed=8 * 2**20, transcendentals=0
         ),
@@ -152,15 +152,15 @@
     restored = (coded.astype(f32) * block_scale).astype(bf16).reshape(micro, own_rows, width)
     received = section_shift(restored, 1)
 
-    restored_c, cot = lax.optimization_barrier((restored, hid_cot[0]))
+    sent = jnp.broadcast_to(received[None], (n_z, micro, own_rows, width)).reshape(-1, own_rows, width)
+    sent, w_own, cot = lax.optimization_barrier((sent, w_up[0], hid_cot[0]))
+    w_other = from_sibling(w_own)
     cot_in = from_sibling(siblings(cot))
-    cot_in, w_own = lax.optimization_barrier((cot_in, w_up[0]))
-    w_other = from_sibling(w_own)
     cot_own = mine(cot)
     cot_all = jnp.where(core == 0, jnp.concatenate([cot_own, cot_in]), jnp.concatenate([cot_in, cot_own]))
 
-    sent = jnp.broadcast_to(received[None], (n_z, micro, own_rows, width)).reshape(-1, own_rows, width)
     by_z = exchange(sent, ("dp", "tensor"), zc_groups)
+    by_z, w_other, cot_all = lax.optimization_barrier((by_z, w_other, cot_all))
     by_z = lax.fori_loop(0, (1 - core) * LAG, lambda i, v: jnp.maximum(v, -jnp.abs(v)), by_z)
     by_xz = gathered(by_z, "tensor", x_groups)
     part, features = forward(core_list, by_xz, w_own, w_other, 256)
@@ -171,16 +171,17 @@
 
     term = backward(core_list, back_all, w_own, w_other, n_z, n_x, 256)
     sum_x = jnp.sum(exchange(term, "tensor", x_groups).astype(f32), axis=0).astype(bf16)
+
+    back_late, _ = lax.optimization_barrier((back_all, term))
+    grad_in = []
+    for piece in jnp.split(features[1], 3, axis=1):
+        grad_in.append(from_sibling(dot(piece, back_late, ((0,), (0,))).astype(bf16)))
+
     returned = exchange(sum_x, ("dp", "tensor"), zc_groups).reshape(n_z, micro, own_rows, width)
     back_input = jnp.sum(returned.astype(f32), axis=0).astype(bf16)
     upstream = section_shift(back_input, -1)
-
-    back_late, _ = lax.optimization_barrier((back_all, term))
-    grad_other = dot(features[1], back_late, ((0,), (0,))).astype(bf16)
-    grad_other, _ = lax.optimization_barrier((grad_other, back_input))
-    grad_in = from_sibling(grad_other)
-    grad = (dot(features[0], back_late, ((0,), (0,))) + grad_in.astype(f32)).astype(bf16)
-    upstream, grad = lax.optimization_barrier((upstream, grad))
+    grad = dot(features[0], back_late, ((0,), (0,))) + jnp.concatenate(grad_in).astype(f32)
+    upstream, grad = lax.optimization_barrier((upstream, grad.astype(bf16)))
     return (upstream[None], grad[None])
 
 

time: 147 us -> 139 us (0.946)
  waiting for transfers between devices: 30.5 us -> 20.9 us
  matrix products: 5.67 us -> 9.89 us
  Pallas kernels: 10 us -> 6.61 us
  local copies, waits for them, and re-layouts: 4.9 us -> 1.79 us
  starting transfers between devices: 50.7 us -> 53.4 us
  blocking collectives: 40.7 us -> 42.3 us
    all_to_all x3, waiting for transfers between devices: 19.7 us -> 13.9 us  [exchange(): lax.all_to_all(value, axis, 0, 0, axis_index_groups=groups, tiled=False)]
    ppermute x3 -> x5, starting transfers between devices: 6.95 us -> 12 us  [from_sibling(): lax.ppermute(value, 'dp', [(d, d ^ 1) for d in range(lax.axis_size('dp'))])]
    dot_general x2 -> x4, matrix products: 5.67 us -> 9.89 us  [dot(): lax.dot_general(a, b, (contract, ((), ())), preferred_element_type=jnp.fl...]
    ppermute x2, waiting for transfers between devices: 9.43 us -> 5.66 us  [section_shift(): lax.ppermute(value, 'pipe', [(s, (s + steps) % n_pipe) for s in range(n_p...]
    pallas_call x1, Pallas kernels: 6.04 us -> 3.38 us  [forward(): pl.pallas_call(forward_kernel, out_shape=(jax.ShapeDtypeStruct((n_z, n_x...]
    unnamed x17 -> x15, local copies, waits for them, and re-layouts: 3.15 us -> 0.67 us
    all_to_all x3, starting transfers between devices: 26.7 us -> 24.5 us  [exchange(): lax.all_to_all(value, axis, 0, 0, axis_index_groups=groups, tiled=False)]
    all_to_all x3, blocking collectives: 40.7 us -> 42.3 us  [exchange(): lax.all_to_all(value, axis, 0, 0, axis_index_groups=groups, tiled=False)]
  transfers between devices with their start and end apart: 8 -> 10, of which waited for: 6 -> 5; matrix products, arithmetic and copies ran while one was open for 4% -> 7% of each run, Pallas kernels for 0% -> 0%
where the time goes in v3:
time: 139 us
  starting transfers between devices  53.4 us (38%)
  blocking collectives  42.3 us (30%)
  waiting for transfers between devices  20.9 us (15%)
  matrix products  9.89 us (7%)
  Pallas kernels  6.61 us (5%)
  other arithmetic  2.74 us (2%)
  local copies, waits for them, and re-layouts  1.79 us (1%)
    all_to_all x3, blocking collectives, exchange(): lax.all_to_all(value, axis, 0, 0, axis_index_groups=groups, tiled=False)  42.3 us
    all_to_all x3, starting transfers between devices, exchange(): lax.all_to_all(value, axis, 0, 0, axis_index_groups=groups, tiled=False)  24.5 us
    ppermute x2, starting transfers between devices, section_shift(): lax.ppermute(value, 'pipe', [(s, (s + steps) % n_pipe) for s in range(n_p...  16.9 us
    all_to_all x3, waiting for transfers between devices, exchange(): lax.all_to_all(value, axis, 0, 0, axis_index_groups=groups, tiled=False)  13.9 us
    ppermute x5, starting transfers between devices, from_sibling(): lax.ppermute(value, 'dp', [(d, d ^ 1) for d in range(lax.axis_size('dp'))])  12 us
    dot_general x4, matrix products, dot(): lax.dot_general(a, b, (contract, ((), ())), preferred_element_type=jnp.fl...  9.89 us
    ppermute x2, waiting for transfers between devices, section_shift(): lax.ppermute(value, 'pipe', [(s, (s + steps) % n_pipe) for s in range(n_p...  5.66 us
    pallas_call x1, Pallas kernels, forward(): pl.pallas_call(forward_kernel, out_shape=(jax.ShapeDtypeStruct((n_z, n_x...  3.38 us
  transfers between devices with their start and end apart: 10, of which 5 were waited for; matrix products, arithmetic and copies ran while one was open for 7% of the time, Pallas kernels for 0%

profile of v3, /device:TPU:1, one launch (start us, length us, event | category | flops | bytes accessed | tf_op | source)
XLA Modules:
  0.0 138.6 jit_solution(9565786306952196799)
XLA Ops:
  0.6 1.0 abs.13
  2.0 9.6 %collective-permute-start = (bf16[2,24,768]{2,1,0:T(8,128)(2,1)S(1)}, bf16[2,24,768]{2,1,0:T(8,128)(2,1)S(1)}, u32[]{:S(2)}, u32[]{:S(2)}) collective-permute-start(bf16[2,24,768]{2,1,0:T(8,128)(2,1)S(1)} %multiply_convert_fusion), channel_id=1, source_target_pairs={{0,128},{128,256},{256,384},{384,0},{1,129},{129,257},{257,385},{3... | collective-permute-start | bytes 221192 | tf_op jit(solution)/shard_map/ppermute | solution.py:20
  11.7 5.7 %collective-permute-done = bf16[2,24,768]{2,1,0:T(8,128)(2,1)S(1)} collective-permute-done((bf16[2,24,768]{2,1,0:T(8,128)(2,1)S(1)}, bf16[2,24,768]{2,1,0:T(8,128)(2,1)S(1)}, u32[]{:S(2)}, u32[]{:S(2)}) %collective-permute-start) | collective-permute-done | bytes 73760 | tf_op jit(solution)/shard_map/ppermute | solution.py:20
  18.1 3.7 %collective-permute-start.1 = (bf16[768,1536]{1,0:T(8,128)(2,1)}, bf16[768,1536]{1,0:T(8,128)(2,1)S(1)}, u32[]{:S(2)}, u32[]{:S(2)}) collective-permute-start(bf16[768,1536]{1,0:T(8,128)(2,1)} %bitcast.36), channel_id=1, source_target_pairs={{0,16},{16,0},{32,48},{48,32},{64,80},{80,64},{96,112},{112,96},{1... | collective-permute-start | bytes 7077896 | tf_op jit(solution)/shard_map/ppermute | solution.py:24
  21.8 7.4 %all-to-all-start = ((bf16[8,24,768]{2,1,0:T(8,128)(2,1)}), bf16[8,24,768]{2,1,0:T(8,128)(2,1)S(1)}, u32[]{:S(2)}, u32[]{:S(2)}) async-start(bf16[8,24,768]{2,1,0:T(8,128)(2,1)} %bitcast.2), calls=%async_computation | async-start | bytes 589824 | tf_op jit(solution)/shard_map/all_to_all | solution.py:36
  29.3 1.9 %collective-permute-start.2 = (bf16[48,1536]{1,0:T(8,128)(2,1)S(1)}, bf16[48,1536]{1,0:T(8,128)(2,1)S(1)}, u32[]{:S(2)}, u32[]{:S(2)}) collective-permute-start(bf16[48,1536]{1,0:T(8,128)(2,1)S(1)} %get-tuple-element.50), channel_id=1, source_target_pairs={{0,16},{16,0},{32,48},{48,32},{64,80},{80,64},{96,112},{112,96},{1... | collective-permute-start | bytes 442376 | tf_op jit(solution)/shard_map/ppermute | solution.py:24
  31.2 1.3 collective-permute-done.2
  32.6 6.0 %all-to-all-done = bf16[8,24,768]{2,1,0:T(8,128)(2,1)S(1)} async-done(((bf16[8,24,768]{2,1,0:T(8,128)(2,1)}), bf16[8,24,768]{2,1,0:T(8,128)(2,1)S(1)}, u32[]{:S(2)}, u32[]{:S(2)}) %all-to-all-start) | async-done | bytes 294944 | tf_op jit(solution)/shard_map/all_to_all | solution.py:36
  38.7 15.0 %all_to_all.30.by_xz_ref = bf16[4,8,24,768]{3,2,1,0:T(8,128)(2,1)S(1)} all-to-all(bf16[4,8,24,768]{3,2,1,0:T(8,128)(2,1)S(1)} %broadcast_in_dim.11), channel_id=1, replica_groups={{0,1,2,3},{4,5,6,7},{8,9,10,11},{12,13,14,15},{16,17,18,19},{20,21,22,2..., dimensions={0} | all-to-all | bytes 2359296 | tf_op jit(solution)/shard_map/all_to_all | solution.py:36
  53.7 3.4 %shard_map.50 = (bf16[4,96,1536]{2,1,0:T(8,128)(2,1)S(1)}, bf16[2,384,768]{2,1,0:T(8,128)(2,1)S(1)}) custom-call(s32[1]{0:T(128)} %bitcast.core_ref, bf16[4,8,24,768]{3,2,1,0:T(8,128)(2,1)S(1)} %all_to_all.30.by_xz_ref, bf16[768,1536]{1,0:T(8,128)(2,1)S(1)} %bitcast.37, bf16[768,1536]{1,0:T(8,128)(2,1)S(1)} %collective-permute-done.1.other_ref), custom_call_target="tpu_custom_call" | custom-call | flops 1811939328 | bytes 10485760 | tf_op jit(solution)/shard_map/pallas_call | solution.py:72
  57.1 14.4 %all_to_all.31 = bf16[4,96,1536]{2,1,0:T(8,128)(2,1)S(1)} all-to-all(bf16[4,96,1536]{2,1,0:T(8,128)(2,1)S(1)} %get-tuple-element.38), channel_id=1, replica_groups={{0,32,64,96},{16,48,80,112},{1,33,65,97},{17,49,81,113},{2,34,66,98},{1..., dimensions={0} | all-to-all | bytes 2359296 | tf_op jit(solution)/shard_map/all_to_all | solution.py:36
  72.2 12.9 %all_to_all.32 = bf16[4,96,1536]{2,1,0:T(8,128)(2,1)S(1)} all-to-all(bf16[4,96,1536]{2,1,0:T(8,128)(2,1)S(1)} %broadcast_in_dim.12), channel_id=1, replica_groups={{0,32,64,96},{16,48,80,112},{1,33,65,97},{17,49,81,113},{2,34,66,98},{1..., dimensions={0} | all-to-all | bytes 2359296 | tf_op jit(solution)/shard_map/all_to_all | solution.py:36
  85.1 3.2 %shard_map.51 = bf16[4,8,24,768]{3,2,1,0:T(8,128)(2,1)} custom-call(s32[1]{0:T(128)} %bitcast.core_ref, bf16[384,1536]{1,0:T(8,128)(2,1)S(1)} %bitcast.31, bf16[768,1536]{1,0:T(8,128)(2,1)S(1)} %bitcast.38, bf16[768,1536]{1,0:T(8,128)(2,1)S(1)} %collective-permute-done.1.other_ref), custom_call_target="tpu_custom_call" | custom-call | flops 1811939328 | bytes 8388608 | tf_op jit(solution)/shard_map/pallas_call | solution.py:112
  88.3 3.7 %all-to-all-start.4 = ((bf16[4,8,24,768]{3,2,1,0:T(8,128)(2,1)}), bf16[4,8,24,768]{3,2,1,0:T(8,128)(2,1)S(1)}, u32[]{:S(2)}, u32[]{:S(2)}) async-start(bf16[4,8,24,768]{3,2,1,0:T(8,128)(2,1)} %shard_map.51), calls=%async_computation.4 | async-start | bytes 2359296 | tf_op jit(solution)/shard_map/all_to_all | solution.py:36
  92.1 1.5 %convolution_convert_fusion = bf16[256,1536]{1,0:T(8,128)(2,1)} fusion(bf16[384,1536]{1,0:T(8,128)(2,1)S(1)} %bitcast.32, bf16[384,768]{1,0:T(8,128)(2,1)S(1)} %slice_bitcast_fusion), kind=kOutput, calls=%fused_computation.2 | convolution fusion | flops 302383104 | bytes 2162688 | tf_op jit(solution)/shard_map/dot_general | solution.py:44
  93.6 1.5 %convolution_convert_fusion.1 = bf16[256,1536]{1,0:T(8,128)(2,1)} fusion(bf16[384,1536]{1,0:T(8,128)(2,1)S(1)} %bitcast.33, bf16[384,768]{1,0:T(8,128)(2,1)S(1)} %slice_bitcast_fusion), kind=kOutput, calls=%fused_computation.3 | convolution fusion | flops 302383104 | bytes 2162688 | tf_op jit(solution)/shard_map/dot_general | solution.py:44
  95.1 7.3 %all-to-all-done.4 = bf16[4,8,24,768]{3,2,1,0:T(8,128)(2,1)S(1)} async-done(((bf16[4,8,24,768]{3,2,1,0:T(8,128)(2,1)}), bf16[4,8,24,768]{3,2,1,0:T(8,128)(2,1)S(1)}, u32[]{:S(2)}, u32[]{:S(2)}) %all-to-all-start.4) | async-done | bytes 1179680 | tf_op jit(solution)/shard_map/all_to_all | solution.py:36
  103.4 13.4 %all-to-all-start.5 = ((bf16[8,24,768]{2,1,0:T(8,128)(2,1)}), bf16[8,24,768]{2,1,0:T(8,128)(2,1)S(1)}, u32[]{:S(2)}, u32[]{:S(2)}) async-start(bf16[8,24,768]{2,1,0:T(8,128)(2,1)} %reduce_sum.34), calls=%async_computation.5 | async-start | bytes 589824 | tf_op jit(solution)/shard_map/all_to_all | solution.py:36
  116.8 2.5 %convolution_convert_fusion.2 = bf16[256,1536]{1,0:T(8,128)(2,1)} fusion(bf16[384,1536]{1,0:T(8,128)(2,1)S(1)} %bitcast.34, bf16[384,768]{1,0:T(8,128)(2,1)} %copy-done.3), kind=kOutput, calls=%fused_computation.4 | convolution fusion | flops 302383104 | bytes 2162688 | tf_op jit(solution)/shard_map/dot_general | solution.py:44
  119.3 2.0 %collective-permute-start.4 = (bf16[256,1536]{1,0:T(8,128)(2,1)}, bf16[256,1536]{1,0:T(8,128)(2,1)}, u32[]{:S(2)}, u32[]{:S(2)}) collective-permute-start(bf16[256,1536]{1,0:T(8,128)(2,1)} %convolution_convert_fusion.2), channel_id=1, source_target_pairs={{0,16},{16,0},{32,48},{48,32},{64,80},{80,64},{96,112},{112,96},{1... | collective-permute-start | bytes 2359304 | tf_op jit(solution)/shard_map/ppermute | solution.py:24
  121.3 2.3 %collective-permute-start.5 = (bf16[256,1536]{1,0:T(8,128)(2,1)}, bf16[256,1536]{1,0:T(8,128)(2,1)}, u32[]{:S(2)}, u32[]{:S(2)}) collective-permute-start(bf16[256,1536]{1,0:T(8,128)(2,1)} %convolution_convert_fusion.1), channel_id=1, source_target_pairs={{0,16},{16,0},{32,48},{48,32},{64,80},{80,64},{96,112},{112,96},{1... | collective-permute-start | bytes 2359304 | tf_op jit(solution)/shard_map/ppermute | solution.py:24
  123.6 2.0 %collective-permute-start.6 = (bf16[256,1536]{1,0:T(8,128)(2,1)S(1)}, bf16[256,1536]{1,0:T(8,128)(2,1)}, u32[]{:S(2)}, u32[]{:S(2)}) collective-permute-start(bf16[256,1536]{1,0:T(8,128)(2,1)S(1)} %copy-done.4), channel_id=1, source_target_pairs={{0,16},{16,0},{32,48},{48,32},{64,80},{80,64},{96,112},{112,96},{1... | collective-permute-start | bytes 2359304 | tf_op jit(solution)/shard_map/ppermute | solution.py:24
  126.2 7.3 %collective-permute-start.3 = (bf16[2,24,768]{2,1,0:T(8,128)(2,1)S(1)}, bf16[2,24,768]{2,1,0:T(8,128)(2,1)S(1)}, u32[]{:S(2)}, u32[]{:S(2)}) collective-permute-start(bf16[2,24,768]{2,1,0:T(8,128)(2,1)S(1)} %reduce_sum.35), channel_id=1, source_target_pairs={{0,384},{128,0},{256,128},{384,256},{1,385},{129,1},{257,129},{385... | collective-permute-start | bytes 221192 | tf_op jit(solution)/shard_map/ppermute | solution.py:20
  133.5 4.4 %add_convert_fusion = bf16[768,1536]{1,0:T(8,128)(2,1)} fusion(bf16[256,1536]{1,0:T(8,128)(2,1)} %collective-permute-done.6, bf16[256,1536]{1,0:T(8,128)(2,1)} %collective-permute-done.5, bf16[256,1536]{1,0:T(8,128)(2,1)} %collective-permute-done.4, bf16[384,1536]{1,0:T(8,128)(2,1)S(1)} %bitcast.35, bf16[2,384,768]{2,1,0:T(8,128)(2,1)S(1)} %copy-done.2), kind=kOutput, calls=%fused_computation.1 | convolution fusion | flops 915406848 | bytes 6488064 | tf_op jit(solution)/shard_map/dot_general | solution.py:44
  (38 shorter events, 4.1 us)
Async XLA Ops:
  0.6 1.3 copy-start.5
  1.7 27.6 %copy-start.6 = (bf16[1,2,48,1536]{3,2,1,0:T(8,128)(2,1)S(1)}, bf16[1,2,48,1536]{3,2,1,0:T(8,128)(2,1)}, u32[]{:S(2)}) copy-start(bf16[1,2,48,1536]{3,2,1,0:T(8,128)(2,1)} %param.6) | copy-start | bytes 884740
  2.0 15.3 %collective-permute-start = (bf16[2,24,768]{2,1,0:T(8,128)(2,1)S(1)}, bf16[2,24,768]{2,1,0:T(8,128)(2,1)S(1)}, u32[]{:S(2)}, u32[]{:S(2)}) collective-permute-start(bf16[2,24,768]{2,1,0:T(8,128)(2,1)S(1)} %multiply_convert_fusion), channel_id=1, source_target_pairs={{0,128},{128,256},{256,384},{384,0},{1,129},{129,257},{257,385},{3... | collective-permute-start | bytes 221192 | tf_op jit(solution)/shard_map/ppermute | solution.py:20
  18.1 20.5 %collective-permute-start.1 = (bf16[768,1536]{1,0:T(8,128)(2,1)}, bf16[768,1536]{1,0:T(8,128)(2,1)S(1)}, u32[]{:S(2)}, u32[]{:S(2)}) collective-permute-start(bf16[768,1536]{1,0:T(8,128)(2,1)} %bitcast.36), channel_id=1, source_target_pairs={{0,16},{16,0},{32,48},{48,32},{64,80},{80,64},{96,112},{112,96},{1... | collective-permute-start | bytes 7077896 | tf_op jit(solution)/shard_map/ppermute | solution.py:24
  21.8 16.8 %all-to-all-start = ((bf16[8,24,768]{2,1,0:T(8,128)(2,1)}), bf16[8,24,768]{2,1,0:T(8,128)(2,1)S(1)}, u32[]{:S(2)}, u32[]{:S(2)}) async-start(bf16[8,24,768]{2,1,0:T(8,128)(2,1)} %bitcast.2), calls=%async_computation | async-start | bytes 589824 | tf_op jit(solution)/shard_map/all_to_all | solution.py:36
  29.3 3.3 %collective-permute-start.2 = (bf16[48,1536]{1,0:T(8,128)(2,1)S(1)}, bf16[48,1536]{1,0:T(8,128)(2,1)S(1)}, u32[]{:S(2)}, u32[]{:S(2)}) collective-permute-start(bf16[48,1536]{1,0:T(8,128)(2,1)S(1)} %get-tuple-element.50), channel_id=1, source_target_pairs={{0,16},{16,0},{32,48},{48,32},{64,80},{80,64},{96,112},{112,96},{1... | collective-permute-start | bytes 442376 | tf_op jit(solution)/shard_map/ppermute | solution.py:24
  38.7 15.1 %copy-start = (bf16[1,768,1536]{2,1,0:T(8,128)(2,1)S(1)}, bf16[1,768,1536]{2,1,0:T(8,128)(2,1)}, u32[]{:S(2)}) copy-start(bf16[1,768,1536]{2,1,0:T(8,128)(2,1)} %param.7) | copy-start | bytes 7077892
  57.1 14.4 %copy-start.1 = (bf16[2,384,768]{2,1,0:T(8,128)(2,1)}, bf16[2,384,768]{2,1,0:T(8,128)(2,1)S(1)}, u32[]{:S(2)}) copy-start(bf16[2,384,768]{2,1,0:T(8,128)(2,1)S(1)} %get-tuple-element.39) | copy-start | bytes 3538948
  88.3 3.7 %copy-start.2 = (bf16[2,384,768]{2,1,0:T(8,128)(2,1)S(1)}, bf16[2,384,768]{2,1,0:T(8,128)(2,1)}, u32[]{:S(2)}) copy-start(bf16[2,384,768]{2,1,0:T(8,128)(2,1)} %copy-done.1) | copy-start | bytes 3538948
  88.3 14.1 %all-to-all-start.4 = ((bf16[4,8,24,768]{3,2,1,0:T(8,128)(2,1)}), bf16[4,8,24,768]{3,2,1,0:T(8,128)(2,1)S(1)}, u32[]{:S(2)}, u32[]{:S(2)}) async-start(bf16[4,8,24,768]{3,2,1,0:T(8,128)(2,1)} %shard_map.51), calls=%async_computation.4 | async-start | bytes 2359296 | tf_op jit(solution)/shard_map/all_to_all | solution.py:36
  92.1 1.5 %copy-start.3 = (bf16[384,768]{1,0:T(8,128)(2,1)}, bf16[384,768]{1,0:T(8,128)(2,1)S(1)}, u32[]{:S(2)}) copy-start(bf16[384,768]{1,0:T(8,128)(2,1)S(1)} %slice_bitcast_fusion) | copy-start | bytes 1769476
  103.4 22.8 %all-to-all-start.5 = ((bf16[8,24,768]{2,1,0:T(8,128)(2,1)}), bf16[8,24,768]{2,1,0:T(8,128)(2,1)S(1)}, u32[]{:S(2)}, u32[]{:S(2)}) async-start(bf16[8,24,768]{2,1,0:T(8,128)(2,1)} %reduce_sum.34), calls=%async_computation.5 | async-start | bytes 589824 | tf_op jit(solution)/shard_map/all_to_all | solution.py:36
  116.8 6.8 %copy-start.4 = (bf16[256,1536]{1,0:T(8,128)(2,1)S(1)}, bf16[256,1536]{1,0:T(8,128)(2,1)}, u32[]{:S(2)}) copy-start(bf16[256,1536]{1,0:T(8,128)(2,1)} %convolution_convert_fusion) | copy-start | bytes 2359300
  119.3 14.2 %collective-permute-start.4 = (bf16[256,1536]{1,0:T(8,128)(2,1)}, bf16[256,1536]{1,0:T(8,128)(2,1)}, u32[]{:S(2)}, u32[]{:S(2)}) collective-permute-start(bf16[256,1536]{1,0:T(8,128)(2,1)} %convolution_convert_fusion.2), channel_id=1, source_target_pairs={{0,16},{16,0},{32,48},{48,32},{64,80},{80,64},{96,112},{112,96},{1... | collective-permute-start | bytes 2359304 | tf_op jit(solution)/shard_map/ppermute | solution.py:24
  121.3 12.2 %collective-permute-start.5 = (bf16[256,1536]{1,0:T(8,128)(2,1)}, bf16[256,1536]{1,0:T(8,128)(2,1)}, u32[]{:S(2)}, u32[]{:S(2)}) collective-permute-start(bf16[256,1536]{1,0:T(8,128)(2,1)} %convolution_convert_fusion.1), channel_id=1, source_target_pairs={{0,16},{16,0},{32,48},{48,32},{64,80},{80,64},{96,112},{112,96},{1... | collective-permute-start | bytes 2359304 | tf_op jit(solution)/shard_map/ppermute | solution.py:24
  123.6 9.9 %collective-permute-start.6 = (bf16[256,1536]{1,0:T(8,128)(2,1)S(1)}, bf16[256,1536]{1,0:T(8,128)(2,1)}, u32[]{:S(2)}, u32[]{:S(2)}) collective-permute-start(bf16[256,1536]{1,0:T(8,128)(2,1)S(1)} %copy-done.4), channel_id=1, source_target_pairs={{0,16},{16,0},{32,48},{48,32},{64,80},{80,64},{96,112},{112,96},{1... | collective-permute-start | bytes 2359304 | tf_op jit(solution)/shard_map/ppermute | solution.py:24
  126.2 11.7 %collective-permute-start.3 = (bf16[2,24,768]{2,1,0:T(8,128)(2,1)S(1)}, bf16[2,24,768]{2,1,0:T(8,128)(2,1)S(1)}, u32[]{:S(2)}, u32[]{:S(2)}) collective-permute-start(bf16[2,24,768]{2,1,0:T(8,128)(2,1)S(1)} %reduce_sum.35), channel_id=1, source_target_pairs={{0,384},{128,0},{256,128},{384,256},{1,385},{129,1},{257,129},{385... | collective-permute-start | bytes 221192 | tf_op jit(solution)/shard_map/ppermute | solution.py:20

commit v4 on v3

--- a/solution.py
+++ b/solution.py
@@ -8,6 +8,8 @@
 BLOCK = 128
 CORES = 2
 LAG = 18
+TILE = 512
+ROWS = 256
 
 
 eps_scale = 1e-06
@@ -47,44 +49,33 @@
 def forward_kernel(core_ref, by_xz_ref, own_ref, other_ref, part_ref, feat_ref):
     f32, bf16 = jnp.float32, jnp.bfloat16
     n_x, n_zc, rows, _ = by_xz_ref.shape
-    core = core_ref[0]
-
-    @pl.when(pl.program_id(0) == 0)
-    def _():
-        for side in range(CORES):
-            block = core if side == 0 else 1 - core
-            for z in range(n_zc // CORES):
-                piece = [by_xz_ref[x, z * CORES + block].astype(f32) for x in range(n_x)]
-                feat_ref[side, pl.ds(z * n_x * rows, n_x * rows)] = jnp.concatenate(piece).astype(bf16)
-
-    part = jnp.dot(feat_ref[0], own_ref[...], preferred_element_type=f32)
-    part += jnp.dot(feat_ref[1], other_ref[...], preferred_element_type=f32)
-    part_ref[...] = part.astype(bf16).reshape(part_ref.shape)
+    for side in range(CORES):
+        block = core_ref[0] if side == 0 else 1 - core_ref[0]
+        for z in range(n_zc // CORES):
+            piece = [by_xz_ref[x, z * CORES + block].astype(f32) for x in range(n_x)]
+            feat_ref[side, pl.ds(z * n_x * rows, n_x * rows)] = jnp.concatenate(piece).astype(bf16)
+    for first in range(0, part_ref.shape[2], TILE):
+        columns = pl.ds(first, TILE)
+        part = jnp.dot(feat_ref[0], own_ref[:, columns], preferred_element_type=f32)
+        part += jnp.dot(feat_ref[1], other_ref[:, columns], preferred_element_type=f32)
+        part_ref[:, :, columns] = part.astype(bf16).reshape(*part_ref.shape[:2], TILE)
 
 
-def forward(core, by_xz, w_own, w_other, tile):
+def forward(core, by_xz, w_own, w_other):
     n_x, n_zc, rows, width = by_xz.shape
     hidden = w_own.shape[1]
     n_z = n_zc // CORES
     tokens = n_z * n_x * rows
-    whole = lambda shape: pl.BlockSpec(shape, lambda j, _: (0,) * len(shape))
-    weights = pl.BlockSpec((width, tile), lambda j, _: (0, j))
+    vmem = pl.BlockSpec(memory_space=pltpu.VMEM)
     return pl.pallas_call(
         forward_kernel,
         out_shape=(
             jax.ShapeDtypeStruct((n_z, n_x * rows, hidden), jnp.bfloat16),
             jax.ShapeDtypeStruct((CORES, tokens, width), jnp.bfloat16),
         ),
-        grid_spec=pltpu.PrefetchScalarGridSpec(
-            num_scalar_prefetch=1,
-            grid=(hidden // tile,),
-            in_specs=[whole(by_xz.shape), weights, weights],
-            out_specs=(
-                pl.BlockSpec((n_z, n_x * rows, tile), lambda j, _: (0, 0, j)),
-                whole((CORES, tokens, width)),
-            ),
-        ),
-        compiler_params=pltpu.CompilerParams(vmem_limit_bytes=16 * 2**20),
+        in_specs=[pl.BlockSpec(memory_space=pltpu.SMEM), vmem, vmem, vmem],
+        out_specs=(vmem, vmem),
+        compiler_params=pltpu.CompilerParams(vmem_limit_bytes=20 * 2**20),
         cost_estimate=pl.CostEstimate(
             flops=2 * tokens * CORES * width * hidden, bytes_accessed=10 * 2**20, transcendentals=0
         ),
@@ -92,33 +83,28 @@
 
 
 def backward_kernel(core_ref, back_ref, own_ref, other_ref, term_ref):
-    n_x, n_zc, rows, _ = term_ref.shape
-    core = core_ref[0]
+    n_x, n_zc, rows, width = term_ref.shape
     for side, w_ref in enumerate((own_ref, other_ref)):
-        block = core if side == 0 else 1 - core
-        term = dot(back_ref[...], w_ref[...], ((1,), (1,)))
-        for z in range(n_zc // CORES):
-            for x in range(n_x):
-                first = (z * n_x + x) * rows
-                term_ref[x, z * CORES + block] = term[first : first + rows].astype(jnp.bfloat16)
+        block = core_ref[0] if side == 0 else 1 - core_ref[0]
+        for tile in range(0, width, ROWS):
+            term = dot(back_ref[...], w_ref[pl.ds(tile, ROWS)], ((1,), (1,)))
+            for z in range(n_zc // CORES):
+                for x in range(n_x):
+                    first = (z * n_x + x) * rows
+                    piece = term[first : first + rows].astype(jnp.bfloat16)
+                    term_ref[x, z * CORES + block, :, pl.ds(tile, ROWS)] = piece
 
 
-def backward(core, back, w_own, w_other, n_z, n_x, tile):
+def backward(core, back, w_own, w_other, n_z, n_x):
     tokens, hidden = back.shape
     width = w_own.shape[0]
-    rows = tokens // n_z // n_x
-    weights = pl.BlockSpec((tile, hidden), lambda j, _: (j, 0))
-    shape = (n_x, n_z * CORES, rows, width)
+    vmem = pl.BlockSpec(memory_space=pltpu.VMEM)
     return pl.pallas_call(
         backward_kernel,
-        out_shape=jax.ShapeDtypeStruct(shape, jnp.bfloat16),
-        grid_spec=pltpu.PrefetchScalarGridSpec(
-            num_scalar_prefetch=1,
-            grid=(width // tile,),
-            in_specs=[pl.BlockSpec((tokens, hidden), lambda j, _: (0, 0)), weights, weights],
-            out_specs=pl.BlockSpec((*shape[:3], tile), lambda j, _: (0, 0, 0, j)),
-        ),
-        compiler_params=pltpu.CompilerParams(vmem_limit_bytes=16 * 2**20),
+        out_shape=jax.ShapeDtypeStruct((n_x, n_z * CORES, tokens // n_z // n_x, width), jnp.bfloat16),
+        in_specs=[pl.BlockSpec(memory_space=pltpu.SMEM), vmem, vmem, vmem],
+        out_specs=vmem,
+        compiler_params=pltpu.CompilerParams(vmem_limit_bytes=20 * 2**20),
         cost_estimate=pl.CostEstimate(
             flops=2 * tokens * CORES * width * hidden, bytes_accessed=8 * 2**20, transcendentals=0
         ),
@@ -163,13 +149,13 @@
     by_z, w_other, cot_all = lax.optimization_barrier((by_z, w_other, cot_all))
     by_z = lax.fori_loop(0, (1 - core) * LAG, lambda i, v: jnp.maximum(v, -jnp.abs(v)), by_z)
     by_xz = gathered(by_z, "tensor", x_groups)
-    part, features = forward(core_list, by_xz, w_own, w_other, 256)
+    part, features = forward(core_list, by_xz, w_own, w_other)
     parts = exchange(part, "dp", y_groups)
     preact = jnp.sum(parts.astype(f32), axis=0)
     back = (cot_all.astype(f32) * gelu_slope(preact)).astype(bf16)
     back_all = gathered(back, "dp", y_groups).reshape(tokens, hidden)
 
-    term = backward(core_list, back_all, w_own, w_other, n_z, n_x, 256)
+    term = backward(core_list, back_all, w_own, w_other, n_z, n_x)
     sum_x = jnp.sum(exchange(term, "tensor", x_groups).astype(f32), axis=0).astype(bf16)
 
     back_late, _ = lax.optimization_barrier((back_all, term))

time: 139 us -> 138 us (level)
  Pallas kernels: 6.61 us -> 5.04 us
    pallas_call x1, Pallas kernels: 3.38 us -> 1.99 us  [forward(): pl.pallas_call(forward_kernel, out_shape=(jax.ShapeDtypeStruct((n_z, n_x...]
where the time goes in v4:
time: 138 us; the launch traced here: 137 us
  starting transfers between devices  53.4 us (39%)
  blocking collectives  42.3 us (31%)
  waiting for transfers between devices  20.9 us (15%)
  matrix products  9.89 us (7%)
  Pallas kernels  5.04 us (4%)
  other arithmetic  2.74 us (2%)
  local copies, waits for them, and re-layouts  1.79 us (1%)
    all_to_all x3, blocking collectives, exchange(): lax.all_to_all(value, axis, 0, 0, axis_index_groups=groups, tiled=False)  42.3 us
    all_to_all x3, starting transfers between devices, exchange(): lax.all_to_all(value, axis, 0, 0, axis_index_groups=groups, tiled=False)  24.5 us
    ppermute x2, starting transfers between devices, section_shift(): lax.ppermute(value, 'pipe', [(s, (s + steps) % n_pipe) for s in range(n_p...  16.9 us
    all_to_all x3, waiting for transfers between devices, exchange(): lax.all_to_all(value, axis, 0, 0, axis_index_groups=groups, tiled=False)  13.9 us
    ppermute x5, starting transfers between devices, from_sibling(): lax.ppermute(value, 'dp', [(d, d ^ 1) for d in range(lax.axis_size('dp'))])  12 us
    dot_general x4, matrix products, dot(): lax.dot_general(a, b, (contract, ((), ())), preferred_element_type=jnp.fl...  9.89 us
    ppermute x2, waiting for transfers between devices, section_shift(): lax.ppermute(value, 'pipe', [(s, (s + steps) % n_pipe) for s in range(n_p...  5.66 us
    pallas_call x1, Pallas kernels, backward(): pl.pallas_call(backward_kernel, out_shape=jax.ShapeDtypeStruct((n_x, n_z...  3.06 us
  transfers between devices with their start and end apart: 10, of which 5 were waited for; matrix products, arithmetic and copies ran while one was open for 7% of the time, Pallas kernels for 0%

profile of v4, /device:TPU:1, one launch (start us, length us, event | category | flops | bytes accessed | tf_op | source)
XLA Modules:
  0.0 137.0 jit_solution(12392863339838409948)
XLA Ops:
  0.6 1.0 abs.13
  2.0 9.6 %collective-permute-start = (bf16[2,24,768]{2,1,0:T(8,128)(2,1)S(1)}, bf16[2,24,768]{2,1,0:T(8,128)(2,1)S(1)}, u32[]{:S(2)}, u32[]{:S(2)}) collective-permute-start(bf16[2,24,768]{2,1,0:T(8,128)(2,1)S(1)} %multiply_convert_fusion), channel_id=1, source_target_pairs={{0,128},{128,256},{256,384},{384,0},{1,129},{129,257},{257,385},{3... | collective-permute-start | bytes 221192 | tf_op jit(solution)/shard_map/ppermute | solution.py:22
  11.7 5.7 %collective-permute-done = bf16[2,24,768]{2,1,0:T(8,128)(2,1)S(1)} collective-permute-done((bf16[2,24,768]{2,1,0:T(8,128)(2,1)S(1)}, bf16[2,24,768]{2,1,0:T(8,128)(2,1)S(1)}, u32[]{:S(2)}, u32[]{:S(2)}) %collective-permute-start) | collective-permute-done | bytes 73760 | tf_op jit(solution)/shard_map/ppermute | solution.py:22
  18.1 3.7 %collective-permute-start.1 = (bf16[768,1536]{1,0:T(8,128)(2,1)}, bf16[768,1536]{1,0:T(8,128)(2,1)S(1)}, u32[]{:S(2)}, u32[]{:S(2)}) collective-permute-start(bf16[768,1536]{1,0:T(8,128)(2,1)} %bitcast.36), channel_id=1, source_target_pairs={{0,16},{16,0},{32,48},{48,32},{64,80},{80,64},{96,112},{112,96},{1... | collective-permute-start | bytes 7077896 | tf_op jit(solution)/shard_map/ppermute | solution.py:26
  21.8 7.4 %all-to-all-start = ((bf16[8,24,768]{2,1,0:T(8,128)(2,1)}), bf16[8,24,768]{2,1,0:T(8,128)(2,1)S(1)}, u32[]{:S(2)}, u32[]{:S(2)}) async-start(bf16[8,24,768]{2,1,0:T(8,128)(2,1)} %bitcast.2), calls=%async_computation | async-start | bytes 589824 | tf_op jit(solution)/shard_map/all_to_all | solution.py:38
  29.3 1.9 %collective-permute-start.2 = (bf16[48,1536]{1,0:T(8,128)(2,1)S(1)}, bf16[48,1536]{1,0:T(8,128)(2,1)S(1)}, u32[]{:S(2)}, u32[]{:S(2)}) collective-permute-start(bf16[48,1536]{1,0:T(8,128)(2,1)S(1)} %get-tuple-element.50), channel_id=1, source_target_pairs={{0,16},{16,0},{32,48},{48,32},{64,80},{80,64},{96,112},{112,96},{1... | collective-permute-start | bytes 442376 | tf_op jit(solution)/shard_map/ppermute | solution.py:26
  31.2 1.3 collective-permute-done.2
  32.6 6.0 %all-to-all-done = bf16[8,24,768]{2,1,0:T(8,128)(2,1)S(1)} async-done(((bf16[8,24,768]{2,1,0:T(8,128)(2,1)}), bf16[8,24,768]{2,1,0:T(8,128)(2,1)S(1)}, u32[]{:S(2)}, u32[]{:S(2)}) %all-to-all-start) | async-done | bytes 294944 | tf_op jit(solution)/shard_map/all_to_all | solution.py:38
  38.7 15.0 %all_to_all.30.by_xz_ref = bf16[4,8,24,768]{3,2,1,0:T(8,128)(2,1)S(1)} all-to-all(bf16[4,8,24,768]{3,2,1,0:T(8,128)(2,1)S(1)} %broadcast_in_dim.11), channel_id=1, replica_groups={{0,1,2,3},{4,5,6,7},{8,9,10,11},{12,13,14,15},{16,17,18,19},{20,21,22,2..., dimensions={0} | all-to-all | bytes 2359296 | tf_op jit(solution)/shard_map/all_to_all | solution.py:38
  53.7 2.0 %shard_map.50 = (bf16[4,96,1536]{2,1,0:T(8,128)(2,1)S(1)}, bf16[2,384,768]{2,1,0:T(8,128)(2,1)S(1)}) custom-call(s32[1]{0:T(128)} %bitcast.core_ref, bf16[4,8,24,768]{3,2,1,0:T(8,128)(2,1)S(1)} %all_to_all.30.by_xz_ref, bf16[768,1536]{1,0:T(8,128)(2,1)S(1)} %bitcast.37, bf16[768,1536]{1,0:T(8,128)(2,1)S(1)} %collective-permute-done.1.other_ref), custom_call_target="tpu_custom_call" | custom-call | flops 1811939328 | bytes 10485760 | tf_op jit(solution)/shard_map/pallas_call | solution.py:70
  55.7 14.4 %all_to_all.31 = bf16[4,96,1536]{2,1,0:T(8,128)(2,1)S(1)} all-to-all(bf16[4,96,1536]{2,1,0:T(8,128)(2,1)S(1)} %get-tuple-element.38), channel_id=1, replica_groups={{0,32,64,96},{16,48,80,112},{1,33,65,97},{17,49,81,113},{2,34,66,98},{1..., dimensions={0} | all-to-all | bytes 2359296 | tf_op jit(solution)/shard_map/all_to_all | solution.py:38
  70.8 12.9 %all_to_all.32 = bf16[4,96,1536]{2,1,0:T(8,128)(2,1)S(1)} all-to-all(bf16[4,96,1536]{2,1,0:T(8,128)(2,1)S(1)} %broadcast_in_dim.12), channel_id=1, replica_groups={{0,32,64,96},{16,48,80,112},{1,33,65,97},{17,49,81,113},{2,34,66,98},{1..., dimensions={0} | all-to-all | bytes 2359296 | tf_op jit(solution)/shard_map/all_to_all | solution.py:38
  83.7 3.1 %shard_map.51 = bf16[4,8,24,768]{3,2,1,0:T(8,128)(2,1)} custom-call(s32[1]{0:T(128)} %bitcast.core_ref, bf16[384,1536]{1,0:T(8,128)(2,1)S(1)} %bitcast.31, bf16[768,1536]{1,0:T(8,128)(2,1)S(1)} %bitcast.38, bf16[768,1536]{1,0:T(8,128)(2,1)S(1)} %collective-permute-done.1.other_ref), custom_call_target="tpu_custom_call" | custom-call | flops 1811939328 | bytes 8388608 | tf_op jit(solution)/shard_map/pallas_call | solution.py:102
  86.8 3.7 %all-to-all-start.4 = ((bf16[4,8,24,768]{3,2,1,0:T(8,128)(2,1)}), bf16[4,8,24,768]{3,2,1,0:T(8,128)(2,1)S(1)}, u32[]{:S(2)}, u32[]{:S(2)}) async-start(bf16[4,8,24,768]{3,2,1,0:T(8,128)(2,1)} %shard_map.51), calls=%async_computation.4 | async-start | bytes 2359296 | tf_op jit(solution)/shard_map/all_to_all | solution.py:38
  90.5 1.5 %convolution_convert_fusion = bf16[256,1536]{1,0:T(8,128)(2,1)} fusion(bf16[384,1536]{1,0:T(8,128)(2,1)S(1)} %bitcast.32, bf16[384,768]{1,0:T(8,128)(2,1)S(1)} %slice_bitcast_fusion), kind=kOutput, calls=%fused_computation.2 | convolution fusion | flops 302383104 | bytes 2162688 | tf_op jit(solution)/shard_map/dot_general | solution.py:46
  92.0 1.5 %convolution_convert_fusion.1 = bf16[256,1536]{1,0:T(8,128)(2,1)} fusion(bf16[384,1536]{1,0:T(8,128)(2,1)S(1)} %bitcast.33, bf16[384,768]{1,0:T(8,128)(2,1)S(1)} %slice_bitcast_fusion), kind=kOutput, calls=%fused_computation.3 | convolution fusion | flops 302383104 | bytes 2162688 | tf_op jit(solution)/shard_map/dot_general | solution.py:46
  93.5 7.3 %all-to-all-done.4 = bf16[4,8,24,768]{3,2,1,0:T(8,128)(2,1)S(1)} async-done(((bf16[4,8,24,768]{3,2,1,0:T(8,128)(2,1)}), bf16[4,8,24,768]{3,2,1,0:T(8,128)(2,1)S(1)}, u32[]{:S(2)}, u32[]{:S(2)}) %all-to-all-start.4) | async-done | bytes 1179680 | tf_op jit(solution)/shard_map/all_to_all | solution.py:38
  101.8 13.4 %all-to-all-start.5 = ((bf16[8,24,768]{2,1,0:T(8,128)(2,1)}), bf16[8,24,768]{2,1,0:T(8,128)(2,1)S(1)}, u32[]{:S(2)}, u32[]{:S(2)}) async-start(bf16[8,24,768]{2,1,0:T(8,128)(2,1)} %reduce_sum.34), calls=%async_computation.5 | async-start | bytes 589824 | tf_op jit(solution)/shard_map/all_to_all | solution.py:38
  115.2 2.5 %convolution_convert_fusion.2 = bf16[256,1536]{1,0:T(8,128)(2,1)} fusion(bf16[384,1536]{1,0:T(8,128)(2,1)S(1)} %bitcast.34, bf16[384,768]{1,0:T(8,128)(2,1)} %copy-done.3), kind=kOutput, calls=%fused_computation.4 | convolution fusion | flops 302383104 | bytes 2162688 | tf_op jit(solution)/shard_map/dot_general | solution.py:46
  117.7 2.0 %collective-permute-start.4 = (bf16[256,1536]{1,0:T(8,128)(2,1)}, bf16[256,1536]{1,0:T(8,128)(2,1)}, u32[]{:S(2)}, u32[]{:S(2)}) collective-permute-start(bf16[256,1536]{1,0:T(8,128)(2,1)} %convolution_convert_fusion.2), channel_id=1, source_target_pairs={{0,16},{16,0},{32,48},{48,32},{64,80},{80,64},{96,112},{112,96},{1... | collective-permute-start | bytes 2359304 | tf_op jit(solution)/shard_map/ppermute | solution.py:26
  119.7 2.3 %collective-permute-start.5 = (bf16[256,1536]{1,0:T(8,128)(2,1)}, bf16[256,1536]{1,0:T(8,128)(2,1)}, u32[]{:S(2)}, u32[]{:S(2)}) collective-permute-start(bf16[256,1536]{1,0:T(8,128)(2,1)} %convolution_convert_fusion.1), channel_id=1, source_target_pairs={{0,16},{16,0},{32,48},{48,32},{64,80},{80,64},{96,112},{112,96},{1... | collective-permute-start | bytes 2359304 | tf_op jit(solution)/shard_map/ppermute | solution.py:26
  122.0 2.0 %collective-permute-start.6 = (bf16[256,1536]{1,0:T(8,128)(2,1)S(1)}, bf16[256,1536]{1,0:T(8,128)(2,1)}, u32[]{:S(2)}, u32[]{:S(2)}) collective-permute-start(bf16[256,1536]{1,0:T(8,128)(2,1)S(1)} %copy-done.4), channel_id=1, source_target_pairs={{0,16},{16,0},{32,48},{48,32},{64,80},{80,64},{96,112},{112,96},{1... | collective-permute-start | bytes 2359304 | tf_op jit(solution)/shard_map/ppermute | solution.py:26
  124.7 7.3 %collective-permute-start.3 = (bf16[2,24,768]{2,1,0:T(8,128)(2,1)S(1)}, bf16[2,24,768]{2,1,0:T(8,128)(2,1)S(1)}, u32[]{:S(2)}, u32[]{:S(2)}) collective-permute-start(bf16[2,24,768]{2,1,0:T(8,128)(2,1)S(1)} %reduce_sum.35), channel_id=1, source_target_pairs={{0,384},{128,0},{256,128},{384,256},{1,385},{129,1},{257,129},{385... | collective-permute-start | bytes 221192 | tf_op jit(solution)/shard_map/ppermute | solution.py:22
  132.0 4.4 %add_convert_fusion = bf16[768,1536]{1,0:T(8,128)(2,1)} fusion(bf16[256,1536]{1,0:T(8,128)(2,1)} %collective-permute-done.6, bf16[256,1536]{1,0:T(8,128)(2,1)} %collective-permute-done.5, bf16[256,1536]{1,0:T(8,128)(2,1)} %collective-permute-done.4, bf16[384,1536]{1,0:T(8,128)(2,1)S(1)} %bitcast.35, bf16[2,384,768]{2,1,0:T(8,128)(2,1)S(1)} %copy-done.2), kind=kOutput, calls=%fused_computation.1 | convolution fusion | flops 915406848 | bytes 6488064 | tf_op jit(solution)/shard_map/dot_general | solution.py:46
  (38 shorter events, 4.1 us)
Async XLA Ops:
  0.6 1.3 copy-start.5
  1.7 27.6 %copy-start.6 = (bf16[1,2,48,1536]{3,2,1,0:T(8,128)(2,1)S(1)}, bf16[1,2,48,1536]{3,2,1,0:T(8,128)(2,1)}, u32[]{:S(2)}) copy-start(bf16[1,2,48,1536]{3,2,1,0:T(8,128)(2,1)} %param.6) | copy-start | bytes 884740
  2.0 15.3 %collective-permute-start = (bf16[2,24,768]{2,1,0:T(8,128)(2,1)S(1)}, bf16[2,24,768]{2,1,0:T(8,128)(2,1)S(1)}, u32[]{:S(2)}, u32[]{:S(2)}) collective-permute-start(bf16[2,24,768]{2,1,0:T(8,128)(2,1)S(1)} %multiply_convert_fusion), channel_id=1, source_target_pairs={{0,128},{128,256},{256,384},{384,0},{1,129},{129,257},{257,385},{3... | collective-permute-start | bytes 221192 | tf_op jit(solution)/shard_map/ppermute | solution.py:22
  18.1 20.5 %collective-permute-start.1 = (bf16[768,1536]{1,0:T(8,128)(2,1)}, bf16[768,1536]{1,0:T(8,128)(2,1)S(1)}, u32[]{:S(2)}, u32[]{:S(2)}) collective-permute-start(bf16[768,1536]{1,0:T(8,128)(2,1)} %bitcast.36), channel_id=1, source_target_pairs={{0,16},{16,0},{32,48},{48,32},{64,80},{80,64},{96,112},{112,96},{1... | collective-permute-start | bytes 7077896 | tf_op jit(solution)/shard_map/ppermute | solution.py:26
  21.8 16.8 %all-to-all-start = ((bf16[8,24,768]{2,1,0:T(8,128)(2,1)}), bf16[8,24,768]{2,1,0:T(8,128)(2,1)S(1)}, u32[]{:S(2)}, u32[]{:S(2)}) async-start(bf16[8,24,768]{2,1,0:T(8,128)(2,1)} %bitcast.2), calls=%async_computation | async-start | bytes 589824 | tf_op jit(solution)/shard_map/all_to_all | solution.py:38
  29.3 3.3 %collective-permute-start.2 = (bf16[48,1536]{1,0:T(8,128)(2,1)S(1)}, bf16[48,1536]{1,0:T(8,128)(2,1)S(1)}, u32[]{:S(2)}, u32[]{:S(2)}) collective-permute-start(bf16[48,1536]{1,0:T(8,128)(2,1)S(1)} %get-tuple-element.50), channel_id=1, source_target_pairs={{0,16},{16,0},{32,48},{48,32},{64,80},{80,64},{96,112},{112,96},{1... | collective-permute-start | bytes 442376 | tf_op jit(solution)/shard_map/ppermute | solution.py:26
  38.7 15.1 %copy-start = (bf16[1,768,1536]{2,1,0:T(8,128)(2,1)S(1)}, bf16[1,768,1536]{2,1,0:T(8,128)(2,1)}, u32[]{:S(2)}) copy-start(bf16[1,768,1536]{2,1,0:T(8,128)(2,1)} %param.7) | copy-start | bytes 7077892
  55.7 14.4 %copy-start.1 = (bf16[2,384,768]{2,1,0:T(8,128)(2,1)}, bf16[2,384,768]{2,1,0:T(8,128)(2,1)S(1)}, u32[]{:S(2)}) copy-start(bf16[2,384,768]{2,1,0:T(8,128)(2,1)S(1)} %get-tuple-element.39) | copy-start | bytes 3538948
  86.8 3.7 %copy-start.2 = (bf16[2,384,768]{2,1,0:T(8,128)(2,1)S(1)}, bf16[2,384,768]{2,1,0:T(8,128)(2,1)}, u32[]{:S(2)}) copy-start(bf16[2,384,768]{2,1,0:T(8,128)(2,1)} %copy-done.1) | copy-start | bytes 3538948
  86.8 14.1 %all-to-all-start.4 = ((bf16[4,8,24,768]{3,2,1,0:T(8,128)(2,1)}), bf16[4,8,24,768]{3,2,1,0:T(8,128)(2,1)S(1)}, u32[]{:S(2)}, u32[]{:S(2)}) async-start(bf16[4,8,24,768]{3,2,1,0:T(8,128)(2,1)} %shard_map.51), calls=%async_computation.4 | async-start | bytes 2359296 | tf_op jit(solution)/shard_map/all_to_all | solution.py:38
  90.5 1.5 %copy-start.3 = (bf16[384,768]{1,0:T(8,128)(2,1)}, bf16[384,768]{1,0:T(8,128)(2,1)S(1)}, u32[]{:S(2)}) copy-start(bf16[384,768]{1,0:T(8,128)(2,1)S(1)} %slice_bitcast_fusion) | copy-start | bytes 1769476
  101.8 22.8 %all-to-all-start.5 = ((bf16[8,24,768]{2,1,0:T(8,128)(2,1)}), bf16[8,24,768]{2,1,0:T(8,128)(2,1)S(1)}, u32[]{:S(2)}, u32[]{:S(2)}) async-start(bf16[8,24,768]{2,1,0:T(8,128)(2,1)} %reduce_sum.34), calls=%async_computation.5 | async-start | bytes 589824 | tf_op jit(solution)/shard_map/all_to_all | solution.py:38
  115.2 6.8 %copy-start.4 = (bf16[256,1536]{1,0:T(8,128)(2,1)S(1)}, bf16[256,1536]{1,0:T(8,128)(2,1)}, u32[]{:S(2)}) copy-start(bf16[256,1536]{1,0:T(8,128)(2,1)} %convolution_convert_fusion) | copy-start | bytes 2359300
  117.7 14.2 %collective-permute-start.4 = (bf16[256,1536]{1,0:T(8,128)(2,1)}, bf16[256,1536]{1,0:T(8,128)(2,1)}, u32[]{:S(2)}, u32[]{:S(2)}) collective-permute-start(bf16[256,1536]{1,0:T(8,128)(2,1)} %convolution_convert_fusion.2), channel_id=1, source_target_pairs={{0,16},{16,0},{32,48},{48,32},{64,80},{80,64},{96,112},{112,96},{1... | collective-permute-start | bytes 2359304 | tf_op jit(solution)/shard_map/ppermute | solution.py:26
  119.7 12.2 %collective-permute-start.5 = (bf16[256,1536]{1,0:T(8,128)(2,1)}, bf16[256,1536]{1,0:T(8,128)(2,1)}, u32[]{:S(2)}, u32[]{:S(2)}) collective-permute-start(bf16[256,1536]{1,0:T(8,128)(2,1)} %convolution_convert_fusion.1), channel_id=1, source_target_pairs={{0,16},{16,0},{32,48},{48,32},{64,80},{80,64},{96,112},{112,96},{1... | collective-permute-start | bytes 2359304 | tf_op jit(solution)/shard_map/ppermute | solution.py:26
  122.0 9.9 %collective-permute-start.6 = (bf16[256,1536]{1,0:T(8,128)(2,1)S(1)}, bf16[256,1536]{1,0:T(8,128)(2,1)}, u32[]{:S(2)}, u32[]{:S(2)}) collective-permute-start(bf16[256,1536]{1,0:T(8,128)(2,1)S(1)} %copy-done.4), channel_id=1, source_target_pairs={{0,16},{16,0},{32,48},{48,32},{64,80},{80,64},{96,112},{112,96},{1... | collective-permute-start | bytes 2359304 | tf_op jit(solution)/shard_map/ppermute | solution.py:26
  124.7 11.7 %collective-permute-start.3 = (bf16[2,24,768]{2,1,0:T(8,128)(2,1)S(1)}, bf16[2,24,768]{2,1,0:T(8,128)(2,1)S(1)}, u32[]{:S(2)}, u32[]{:S(2)}) collective-permute-start(bf16[2,24,768]{2,1,0:T(8,128)(2,1)S(1)} %reduce_sum.35), channel_id=1, source_target_pairs={{0,384},{128,0},{256,128},{384,256},{1,385},{129,1},{257,129},{385... | collective-permute-start | bytes 221192 | tf_op jit(solution)/shard_map/ppermute | solution.py:22

commit v5 on v4

--- a/solution.py
+++ b/solution.py
@@ -109,6 +109,25 @@
             flops=2 * tokens * CORES * width * hidden, bytes_accessed=8 * 2**20, transcendentals=0
         ),
     )(core, back, w_own, w_other)
+
+
+def sum_kernel(parts_ref, sum_ref):
+    total = parts_ref[0].astype(jnp.float32)
+    for part in range(1, parts_ref.shape[0]):
+        total += parts_ref[part].astype(jnp.float32)
+    sum_ref[...] = total.astype(jnp.bfloat16)
+
+
+def sum_parts(parts):
+    vmem = pl.BlockSpec(memory_space=pltpu.VMEM)
+    return pl.pallas_call(
+        sum_kernel,
+        out_shape=jax.ShapeDtypeStruct(parts.shape[1:], parts.dtype),
+        in_specs=[vmem],
+        out_specs=vmem,
+        compiler_params=pltpu.CompilerParams(vmem_limit_bytes=16 * 2**20),
+        cost_estimate=pl.CostEstimate(flops=parts.size, bytes_accessed=2 * parts.size, transcendentals=0),
+    )(parts)
 
 
 def local(x_prev, hid_cot, w_up):
@@ -156,7 +175,7 @@
     back_all = gathered(back, "dp", y_groups).reshape(tokens, hidden)
 
     term = backward(core_list, back_all, w_own, w_other, n_z, n_x)
-    sum_x = jnp.sum(exchange(term, "tensor", x_groups).astype(f32), axis=0).astype(bf16)
+    sum_x = sum_parts(exchange(term, "tensor", x_groups))
 
     back_late, _ = lax.optimization_barrier((back_all, term))
     grad_in = []

time: 138 us -> 138 us (level)
  no operation moved by 1% of the time
where the time goes in v5:
time: 138 us; the launch traced here: 137 us
  starting transfers between devices  53.4 us (39%)
  blocking collectives  42.3 us (31%)
  waiting for transfers between devices  20.9 us (15%)
  matrix products  9.93 us (7%)
  Pallas kernels  5.9 us (4%)
  other arithmetic  1.8 us (1%)
  local copies, waits for them, and re-layouts  1.79 us (1%)
    all_to_all x3, blocking collectives, exchange(): lax.all_to_all(value, axis, 0, 0, axis_index_groups=groups, tiled=False)  42.3 us
    all_to_all x3, starting transfers between devices, exchange(): lax.all_to_all(value, axis, 0, 0, axis_index_groups=groups, tiled=False)  24.5 us
    ppermute x2, starting transfers between devices, section_shift(): lax.ppermute(value, 'pipe', [(s, (s + steps) % n_pipe) for s in range(n_p...  16.9 us
    all_to_all x3, waiting for transfers between devices, exchange(): lax.all_to_all(value, axis, 0, 0, axis_index_groups=groups, tiled=False)  13.9 us
    ppermute x5, starting transfers between devices, from_sibling(): lax.ppermute(value, 'dp', [(d, d ^ 1) for d in range(lax.axis_size('dp'))])  12 us
    dot_general x4, matrix products, dot(): lax.dot_general(a, b, (contract, ((), ())), preferred_element_type=jnp.fl...  9.93 us
    ppermute x2, waiting for transfers between devices, section_shift(): lax.ppermute(value, 'pipe', [(s, (s + steps) % n_pipe) for s in range(n_p...  5.66 us
    pallas_call x1, Pallas kernels, backward(): pl.pallas_call(backward_kernel, out_shape=jax.ShapeDtypeStruct((n_x, n_z...  3.06 us
  transfers between devices with their start and end apart: 10, of which 5 were waited for; matrix products, arithmetic and copies ran while one was open for 7% of the time, Pallas kernels for 0%

profile of v5, /device:TPU:1, one launch (start us, length us, event | category | flops | bytes accessed | tf_op | source)
XLA Modules:
  0.0 136.9 jit_solution(17026984187064054592)
XLA Ops:
  0.6 1.0 abs.13
  2.0 9.6 %collective-permute-start = (bf16[2,24,768]{2,1,0:T(8,128)(2,1)S(1)}, bf16[2,24,768]{2,1,0:T(8,128)(2,1)S(1)}, u32[]{:S(2)}, u32[]{:S(2)}) collective-permute-start(bf16[2,24,768]{2,1,0:T(8,128)(2,1)S(1)} %multiply_convert_fusion), channel_id=1, source_target_pairs={{0,128},{128,256},{256,384},{384,0},{1,129},{129,257},{257,385},{3... | collective-permute-start | bytes 221192 | tf_op jit(solution)/shard_map/ppermute | solution.py:22
  11.7 5.7 %collective-permute-done = bf16[2,24,768]{2,1,0:T(8,128)(2,1)S(1)} collective-permute-done((bf16[2,24,768]{2,1,0:T(8,128)(2,1)S(1)}, bf16[2,24,768]{2,1,0:T(8,128)(2,1)S(1)}, u32[]{:S(2)}, u32[]{:S(2)}) %collective-permute-start) | collective-permute-done | bytes 73760 | tf_op jit(solution)/shard_map/ppermute | solution.py:22
  18.1 3.7 %collective-permute-start.1 = (bf16[768,1536]{1,0:T(8,128)(2,1)}, bf16[768,1536]{1,0:T(8,128)(2,1)S(1)}, u32[]{:S(2)}, u32[]{:S(2)}) collective-permute-start(bf16[768,1536]{1,0:T(8,128)(2,1)} %bitcast.36), channel_id=1, source_target_pairs={{0,16},{16,0},{32,48},{48,32},{64,80},{80,64},{96,112},{112,96},{1... | collective-permute-start | bytes 7077896 | tf_op jit(solution)/shard_map/ppermute | solution.py:26
  21.8 7.4 %all-to-all-start = ((bf16[8,24,768]{2,1,0:T(8,128)(2,1)}), bf16[8,24,768]{2,1,0:T(8,128)(2,1)S(1)}, u32[]{:S(2)}, u32[]{:S(2)}) async-start(bf16[8,24,768]{2,1,0:T(8,128)(2,1)} %bitcast.2), calls=%async_computation | async-start | bytes 589824 | tf_op jit(solution)/shard_map/all_to_all | solution.py:38
  29.3 1.9 %collective-permute-start.2 = (bf16[48,1536]{1,0:T(8,128)(2,1)S(1)}, bf16[48,1536]{1,0:T(8,128)(2,1)S(1)}, u32[]{:S(2)}, u32[]{:S(2)}) collective-permute-start(bf16[48,1536]{1,0:T(8,128)(2,1)S(1)} %get-tuple-element.50), channel_id=1, source_target_pairs={{0,16},{16,0},{32,48},{48,32},{64,80},{80,64},{96,112},{112,96},{1... | collective-permute-start | bytes 442376 | tf_op jit(solution)/shard_map/ppermute | solution.py:26
  31.2 1.3 collective-permute-done.2
  32.6 6.0 %all-to-all-done = bf16[8,24,768]{2,1,0:T(8,128)(2,1)S(1)} async-done(((bf16[8,24,768]{2,1,0:T(8,128)(2,1)}), bf16[8,24,768]{2,1,0:T(8,128)(2,1)S(1)}, u32[]{:S(2)}, u32[]{:S(2)}) %all-to-all-start) | async-done | bytes 294944 | tf_op jit(solution)/shard_map/all_to_all | solution.py:38
  38.7 15.0 %all_to_all.30.by_xz_ref = bf16[4,8,24,768]{3,2,1,0:T(8,128)(2,1)S(1)} all-to-all(bf16[4,8,24,768]{3,2,1,0:T(8,128)(2,1)S(1)} %broadcast_in_dim.11), channel_id=1, replica_groups={{0,1,2,3},{4,5,6,7},{8,9,10,11},{12,13,14,15},{16,17,18,19},{20,21,22,2..., dimensions={0} | all-to-all | bytes 2359296 | tf_op jit(solution)/shard_map/all_to_all | solution.py:38
  53.7 2.0 %shard_map.50 = (bf16[4,96,1536]{2,1,0:T(8,128)(2,1)S(1)}, bf16[2,384,768]{2,1,0:T(8,128)(2,1)S(1)}) custom-call(s32[1]{0:T(128)} %bitcast.core_ref, bf16[4,8,24,768]{3,2,1,0:T(8,128)(2,1)S(1)} %all_to_all.30.by_xz_ref, bf16[768,1536]{1,0:T(8,128)(2,1)S(1)} %bitcast.37, bf16[768,1536]{1,0:T(8,128)(2,1)S(1)} %collective-permute-done.1.other_ref), custom_call_target="tpu_custom_call" | custom-call | flops 1811939328 | bytes 10485760 | tf_op jit(solution)/shard_map/pallas_call | solution.py:70
  55.7 14.4 %all_to_all.31 = bf16[4,96,1536]{2,1,0:T(8,128)(2,1)S(1)} all-to-all(bf16[4,96,1536]{2,1,0:T(8,128)(2,1)S(1)} %get-tuple-element.38), channel_id=1, replica_groups={{0,32,64,96},{16,48,80,112},{1,33,65,97},{17,49,81,113},{2,34,66,98},{1..., dimensions={0} | all-to-all | bytes 2359296 | tf_op jit(solution)/shard_map/all_to_all | solution.py:38
  70.8 12.9 %all_to_all.32 = bf16[4,96,1536]{2,1,0:T(8,128)(2,1)S(1)} all-to-all(bf16[4,96,1536]{2,1,0:T(8,128)(2,1)S(1)} %broadcast_in_dim.12), channel_id=1, replica_groups={{0,32,64,96},{16,48,80,112},{1,33,65,97},{17,49,81,113},{2,34,66,98},{1..., dimensions={0} | all-to-all | bytes 2359296 | tf_op jit(solution)/shard_map/all_to_all | solution.py:38
  83.7 3.1 %shard_map.51 = bf16[4,8,24,768]{3,2,1,0:T(8,128)(2,1)} custom-call(s32[1]{0:T(128)} %bitcast.core_ref, bf16[384,1536]{1,0:T(8,128)(2,1)S(1)} %bitcast.31, bf16[768,1536]{1,0:T(8,128)(2,1)S(1)} %bitcast.38, bf16[768,1536]{1,0:T(8,128)(2,1)S(1)} %collective-permute-done.1.other_ref), custom_call_target="tpu_custom_call" | custom-call | flops 1811939328 | bytes 8388608 | tf_op jit(solution)/shard_map/pallas_call | solution.py:102
  86.8 3.7 %all-to-all-start.4 = ((bf16[4,8,24,768]{3,2,1,0:T(8,128)(2,1)}), bf16[4,8,24,768]{3,2,1,0:T(8,128)(2,1)S(1)}, u32[]{:S(2)}, u32[]{:S(2)}) async-start(bf16[4,8,24,768]{3,2,1,0:T(8,128)(2,1)} %shard_map.51), calls=%async_computation.4 | async-start | bytes 2359296 | tf_op jit(solution)/shard_map/all_to_all | solution.py:38
  90.5 1.5 %convolution_convert_fusion = bf16[256,1536]{1,0:T(8,128)(2,1)} fusion(bf16[384,1536]{1,0:T(8,128)(2,1)S(1)} %bitcast.32, bf16[384,768]{1,0:T(8,128)(2,1)S(1)} %slice_bitcast_fusion), kind=kOutput, calls=%fused_computation.2 | convolution fusion | flops 302383104 | bytes 2162688 | tf_op jit(solution)/shard_map/dot_general | solution.py:46
  92.0 1.5 %convolution_convert_fusion.1 = bf16[256,1536]{1,0:T(8,128)(2,1)} fusion(bf16[384,1536]{1,0:T(8,128)(2,1)S(1)} %bitcast.33, bf16[384,768]{1,0:T(8,128)(2,1)S(1)} %slice_bitcast_fusion), kind=kOutput, calls=%fused_computation.3 | convolution fusion | flops 302383104 | bytes 2162688 | tf_op jit(solution)/shard_map/dot_general | solution.py:46
  93.5 7.3 %all-to-all-done.4.parts_ref = bf16[4,8,24,768]{3,2,1,0:T(8,128)(2,1)S(1)} async-done(((bf16[4,8,24,768]{3,2,1,0:T(8,128)(2,1)}), bf16[4,8,24,768]{3,2,1,0:T(8,128)(2,1)S(1)}, u32[]{:S(2)}, u32[]{:S(2)}) %all-to-all-start.4) | async-done | bytes 1179680 | tf_op jit(solution)/shard_map/all_to_all | solution.py:38
  101.7 13.4 %all-to-all-start.5 = ((bf16[8,24,768]{2,1,0:T(8,128)(2,1)}), bf16[8,24,768]{2,1,0:T(8,128)(2,1)S(1)}, u32[]{:S(2)}, u32[]{:S(2)}) async-start(bf16[8,24,768]{2,1,0:T(8,128)(2,1)} %shard_map.52), calls=%async_computation.5 | async-start | bytes 589824 | tf_op jit(solution)/shard_map/all_to_all | solution.py:38
  115.1 2.5 %convolution_convert_fusion.2 = bf16[256,1536]{1,0:T(8,128)(2,1)} fusion(bf16[384,1536]{1,0:T(8,128)(2,1)S(1)} %bitcast.34, bf16[384,768]{1,0:T(8,128)(2,1)} %copy-done.3), kind=kOutput, calls=%fused_computation.4 | convolution fusion | flops 302383104 | bytes 2162688 | tf_op jit(solution)/shard_map/dot_general | solution.py:46
  117.6 2.0 %collective-permute-start.4 = (bf16[256,1536]{1,0:T(8,128)(2,1)}, bf16[256,1536]{1,0:T(8,128)(2,1)}, u32[]{:S(2)}, u32[]{:S(2)}) collective-permute-start(bf16[256,1536]{1,0:T(8,128)(2,1)} %convolution_convert_fusion.2), channel_id=1, source_target_pairs={{0,16},{16,0},{32,48},{48,32},{64,80},{80,64},{96,112},{112,96},{1... | collective-permute-start | bytes 2359304 | tf_op jit(solution)/shard_map/ppermute | solution.py:26
  119.6 2.3 %collective-permute-start.5 = (bf16[256,1536]{1,0:T(8,128)(2,1)}, bf16[256,1536]{1,0:T(8,128)(2,1)}, u32[]{:S(2)}, u32[]{:S(2)}) collective-permute-start(bf16[256,1536]{1,0:T(8,128)(2,1)} %convolution_convert_fusion.1), channel_id=1, source_target_pairs={{0,16},{16,0},{32,48},{48,32},{64,80},{80,64},{96,112},{112,96},{1... | collective-permute-start | bytes 2359304 | tf_op jit(solution)/shard_map/ppermute | solution.py:26
  122.0 2.0 %collective-permute-start.6 = (bf16[256,1536]{1,0:T(8,128)(2,1)S(1)}, bf16[256,1536]{1,0:T(8,128)(2,1)}, u32[]{:S(2)}, u32[]{:S(2)}) collective-permute-start(bf16[256,1536]{1,0:T(8,128)(2,1)S(1)} %copy-done.4), channel_id=1, source_target_pairs={{0,16},{16,0},{32,48},{48,32},{64,80},{80,64},{96,112},{112,96},{1... | collective-permute-start | bytes 2359304 | tf_op jit(solution)/shard_map/ppermute | solution.py:26
  124.6 7.3 %collective-permute-start.3 = (bf16[2,24,768]{2,1,0:T(8,128)(2,1)S(1)}, bf16[2,24,768]{2,1,0:T(8,128)(2,1)S(1)}, u32[]{:S(2)}, u32[]{:S(2)}) collective-permute-start(bf16[2,24,768]{2,1,0:T(8,128)(2,1)S(1)} %reduce_sum.22), channel_id=1, source_target_pairs={{0,384},{128,0},{256,128},{384,256},{1,385},{129,1},{257,129},{385... | collective-permute-start | bytes 221192 | tf_op jit(solution)/shard_map/ppermute | solution.py:22
  131.9 4.4 %add_convert_fusion = bf16[768,1536]{1,0:T(8,128)(2,1)} fusion(bf16[256,1536]{1,0:T(8,128)(2,1)} %collective-permute-done.6, bf16[256,1536]{1,0:T(8,128)(2,1)} %collective-permute-done.5, bf16[256,1536]{1,0:T(8,128)(2,1)} %collective-permute-done.4, bf16[384,1536]{1,0:T(8,128)(2,1)S(1)} %bitcast.35, bf16[2,384,768]{2,1,0:T(8,128)(2,1)S(1)} %copy-done.2), kind=kOutput, calls=%fused_computation.1 | convolution fusion | flops 915406848 | bytes 6488064 | tf_op jit(solution)/shard_map/dot_general | solution.py:46
  (38 shorter events, 4.0 us)
Async XLA Ops:
  0.6 1.3 copy-start.5
  1.7 27.6 %copy-start.6 = (bf16[1,2,48,1536]{3,2,1,0:T(8,128)(2,1)S(1)}, bf16[1,2,48,1536]{3,2,1,0:T(8,128)(2,1)}, u32[]{:S(2)}) copy-start(bf16[1,2,48,1536]{3,2,1,0:T(8,128)(2,1)} %param.6) | copy-start | bytes 884740
  2.0 15.3 %collective-permute-start = (bf16[2,24,768]{2,1,0:T(8,128)(2,1)S(1)}, bf16[2,24,768]{2,1,0:T(8,128)(2,1)S(1)}, u32[]{:S(2)}, u32[]{:S(2)}) collective-permute-start(bf16[2,24,768]{2,1,0:T(8,128)(2,1)S(1)} %multiply_convert_fusion), channel_id=1, source_target_pairs={{0,128},{128,256},{256,384},{384,0},{1,129},{129,257},{257,385},{3... | collective-permute-start | bytes 221192 | tf_op jit(solution)/shard_map/ppermute | solution.py:22
  18.1 20.5 %collective-permute-start.1 = (bf16[768,1536]{1,0:T(8,128)(2,1)}, bf16[768,1536]{1,0:T(8,128)(2,1)S(1)}, u32[]{:S(2)}, u32[]{:S(2)}) collective-permute-start(bf16[768,1536]{1,0:T(8,128)(2,1)} %bitcast.36), channel_id=1, source_target_pairs={{0,16},{16,0},{32,48},{48,32},{64,80},{80,64},{96,112},{112,96},{1... | collective-permute-start | bytes 7077896 | tf_op jit(solution)/shard_map/ppermute | solution.py:26
  21.8 16.8 %all-to-all-start = ((bf16[8,24,768]{2,1,0:T(8,128)(2,1)}), bf16[8,24,768]{2,1,0:T(8,128)(2,1)S(1)}, u32[]{:S(2)}, u32[]{:S(2)}) async-start(bf16[8,24,768]{2,1,0:T(8,128)(2,1)} %bitcast.2), calls=%async_computation | async-start | bytes 589824 | tf_op jit(solution)/shard_map/all_to_all | solution.py:38
  29.3 3.3 %collective-permute-start.2 = (bf16[48,1536]{1,0:T(8,128)(2,1)S(1)}, bf16[48,1536]{1,0:T(8,128)(2,1)S(1)}, u32[]{:S(2)}, u32[]{:S(2)}) collective-permute-start(bf16[48,1536]{1,0:T(8,128)(2,1)S(1)} %get-tuple-element.50), channel_id=1, source_target_pairs={{0,16},{16,0},{32,48},{48,32},{64,80},{80,64},{96,112},{112,96},{1... | collective-permute-start | bytes 442376 | tf_op jit(solution)/shard_map/ppermute | solution.py:26
  38.7 15.1 %copy-start = (bf16[1,768,1536]{2,1,0:T(8,128)(2,1)S(1)}, bf16[1,768,1536]{2,1,0:T(8,128)(2,1)}, u32[]{:S(2)}) copy-start(bf16[1,768,1536]{2,1,0:T(8,128)(2,1)} %param.7) | copy-start | bytes 7077892
  55.7 14.4 %copy-start.1 = (bf16[2,384,768]{2,1,0:T(8,128)(2,1)}, bf16[2,384,768]{2,1,0:T(8,128)(2,1)S(1)}, u32[]{:S(2)}) copy-start(bf16[2,384,768]{2,1,0:T(8,128)(2,1)S(1)} %get-tuple-element.39) | copy-start | bytes 3538948
  86.8 3.7 %copy-start.2 = (bf16[2,384,768]{2,1,0:T(8,128)(2,1)S(1)}, bf16[2,384,768]{2,1,0:T(8,128)(2,1)}, u32[]{:S(2)}) copy-start(bf16[2,384,768]{2,1,0:T(8,128)(2,1)} %copy-done.1) | copy-start | bytes 3538948
  86.8 14.1 %all-to-all-start.4 = ((bf16[4,8,24,768]{3,2,1,0:T(8,128)(2,1)}), bf16[4,8,24,768]{3,2,1,0:T(8,128)(2,1)S(1)}, u32[]{:S(2)}, u32[]{:S(2)}) async-start(bf16[4,8,24,768]{3,2,1,0:T(8,128)(2,1)} %shard_map.51), calls=%async_computation.4 | async-start | bytes 2359296 | tf_op jit(solution)/shard_map/all_to_all | solution.py:38
  90.5 1.5 %copy-start.3 = (bf16[384,768]{1,0:T(8,128)(2,1)}, bf16[384,768]{1,0:T(8,128)(2,1)S(1)}, u32[]{:S(2)}) copy-start(bf16[384,768]{1,0:T(8,128)(2,1)S(1)} %slice_bitcast_fusion) | copy-start | bytes 1769476
  101.7 22.8 %all-to-all-start.5 = ((bf16[8,24,768]{2,1,0:T(8,128)(2,1)}), bf16[8,24,768]{2,1,0:T(8,128)(2,1)S(1)}, u32[]{:S(2)}, u32[]{:S(2)}) async-start(bf16[8,24,768]{2,1,0:T(8,128)(2,1)} %shard_map.52), calls=%async_computation.5 | async-start | bytes 589824 | tf_op jit(solution)/shard_map/all_to_all | solution.py:38
  115.1 6.8 %copy-start.4 = (bf16[256,1536]{1,0:T(8,128)(2,1)S(1)}, bf16[256,1536]{1,0:T(8,128)(2,1)}, u32[]{:S(2)}) copy-start(bf16[256,1536]{1,0:T(8,128)(2,1)} %convolution_convert_fusion) | copy-start | bytes 2359300
  117.6 14.2 %collective-permute-start.4 = (bf16[256,1536]{1,0:T(8,128)(2,1)}, bf16[256,1536]{1,0:T(8,128)(2,1)}, u32[]{:S(2)}, u32[]{:S(2)}) collective-permute-start(bf16[256,1536]{1,0:T(8,128)(2,1)} %convolution_convert_fusion.2), channel_id=1, source_target_pairs={{0,16},{16,0},{32,48},{48,32},{64,80},{80,64},{96,112},{112,96},{1... | collective-permute-start | bytes 2359304 | tf_op jit(solution)/shard_map/ppermute | solution.py:26
  119.6 12.2 %collective-permute-start.5 = (bf16[256,1536]{1,0:T(8,128)(2,1)}, bf16[256,1536]{1,0:T(8,128)(2,1)}, u32[]{:S(2)}, u32[]{:S(2)}) collective-permute-start(bf16[256,1536]{1,0:T(8,128)(2,1)} %convolution_convert_fusion.1), channel_id=1, source_target_pairs={{0,16},{16,0},{32,48},{48,32},{64,80},{80,64},{96,112},{112,96},{1... | collective-permute-start | bytes 2359304 | tf_op jit(solution)/shard_map/ppermute | solution.py:26
  122.0 9.9 %collective-permute-start.6 = (bf16[256,1536]{1,0:T(8,128)(2,1)S(1)}, bf16[256,1536]{1,0:T(8,128)(2,1)}, u32[]{:S(2)}, u32[]{:S(2)}) collective-permute-start(bf16[256,1536]{1,0:T(8,128)(2,1)S(1)} %copy-done.4), channel_id=1, source_target_pairs={{0,16},{16,0},{32,48},{48,32},{64,80},{80,64},{96,112},{112,96},{1... | collective-permute-start | bytes 2359304 | tf_op jit(solution)/shard_map/ppermute | solution.py:26
  124.6 11.7 %collective-permute-start.3 = (bf16[2,24,768]{2,1,0:T(8,128)(2,1)S(1)}, bf16[2,24,768]{2,1,0:T(8,128)(2,1)S(1)}, u32[]{:S(2)}, u32[]{:S(2)}) collective-permute-start(bf16[2,24,768]{2,1,0:T(8,128)(2,1)S(1)} %reduce_sum.22), channel_id=1, source_target_pairs={{0,384},{128,0},{256,128},{384,256},{1,385},{129,1},{257,129},{385... | collective-permute-start | bytes 221192 | tf_op jit(solution)/shard_map/ppermute | solution.py:22
